TPU v7x, 128 devices: a whole 4x4x4 slice. The times are simulated.
128 devices in a mesh: row: 8 (over z, core), col: 16 (over y, x).
Axes of the slice: x: 4, y: 4, z: 4, core: 2. Of those that a mesh axis runs over, the one named last changes fastest.
Arguments:
- current: float32 [4096, 128], P(('row', 'col')), may hold values from -6 to 6
- owner: int32 [4096], P(('row', 'col')), may hold values from 0 to 127, as said below
- voxel: int32 [4096, 128], P(('row', 'col')), may hold values from -1 to 65535, as said below
- material: int32 [4096, 128], P(('row', 'col')), may hold values from 0 to 7
- resist: float32 [8], replicated, may hold values from 0.5 to 4
- green: float32 [3, 2, 4096, 4096], P(None, None, ('row', 'col')), may hold values from -36 to 36
Outputs:
- image_rows: float32 [4096, 128], P(('row', 'col'))
Inputs may be any that keep to these rules, and one draw needn't show every extreme that they name: The 32 blocks of one device name 32 different owners; one owner is named by a block of every device. `voxel`: A block's live rows come first, the rest hold -1; each block has between three quarters of 128 and 128 live rows, and every device has a block with 128 live rows. No two live rows of all blocks name the same cell of the same owner.
All inputs are finite; a program needn't handle non-finite values.
Results may differ from a plain program's by a relative error of at most 0.00005.
Values sent between devices are 32-bit elements; how exact they have to be, the bound alone decides.
A program may use at most 256 MiB of HBM per device.

v0:
```python
import math

import jax
import jax.numpy as jnp
from jax import lax
from jax.sharding import PartitionSpec as P

highest = lax.Precision.HIGHEST


def angle_tables(length, extent):
    row_ids = lax.broadcasted_iota(jnp.int32, (extent, length), 0)
    col_ids = lax.broadcasted_iota(jnp.int32, (extent, length), 1)
    angles = (row_ids * col_ids % length).astype(jnp.float32) * (2.0 * math.pi / length)
    return (jnp.cos(angles), jnp.sin(angles))


def forward_rows(matrix, cos_table, sin_table, length):
    block_cols = min(length, 512)
    real_parts = []
    imag_parts = []
    for offset in range(0, length, block_cols):
        cosine = cos_table[:, offset : offset + block_cols]
        sine_part = sin_table[:, offset : offset + block_cols]
        real_parts.append(jnp.dot(matrix, cosine, precision=highest))
        imag_parts.append(-jnp.dot(matrix, sine_part, precision=highest))
    return (jnp.concatenate(real_parts, axis=1), jnp.concatenate(imag_parts, axis=1))


def forward_columns(pencil, cos_table, sin_table, length):
    block_cols = min(length, 512)
    cosine_parts = []
    sine_parts = []
    contract = (((0,), (0,)), ((), ()))
    for offset in range(0, length, block_cols):
        cosine = cos_table[:, offset : offset + block_cols]
        sine_part = sin_table[:, offset : offset + block_cols]
        cosine_parts.append(lax.dot_general(pencil, cosine, contract, precision=highest))
        sine_parts.append(lax.dot_general(pencil, sine_part, contract, precision=highest))
    return (jnp.concatenate(cosine_parts, axis=1), jnp.concatenate(sine_parts, axis=1))


def inverse_columns(spectra, cos_table, sin_table, length, extent):
    block_cols = min(length, 512)
    contract = (((1,), (1,)), ((), ()))
    running_cos = jnp.zeros((extent, spectra.shape[0]), jnp.float32)
    running_sin = jnp.zeros((extent, spectra.shape[0]), jnp.float32)
    for offset in range(0, length, block_cols):
        cosine = cos_table[:, offset : offset + block_cols]
        sine_part = sin_table[:, offset : offset + block_cols]
        section = spectra[:, offset : offset + block_cols]
        running_cos = running_cos + lax.dot_general(cosine, section, contract, precision=highest)
        running_sin = running_sin + lax.dot_general(sine_part, section, contract, precision=highest)
    return (running_cos, running_sin)


def inverse_rows(real_part, imag_part, cos_table, sin_table, length, extent):
    block_cols = min(length, 512)
    contract = (((1,), (1,)), ((), ()))
    running = jnp.zeros((real_part.shape[0], extent), jnp.float32)
    for offset in range(0, length, block_cols):
        cosine = cos_table[:, offset : offset + block_cols]
        sine_part = sin_table[:, offset : offset + block_cols]
        running = running + lax.dot_general(
            real_part[:, offset : offset + block_cols], cosine, contract, precision=highest
        )
        running = running - lax.dot_general(
            imag_part[:, offset : offset + block_cols], sine_part, contract, precision=highest
        )
    return running


def shards(current, owner, voxel, material, resist, green):
    row_count = lax.axis_size("row")
    col_count = lax.axis_size("col")
    devices = row_count * col_count
    block_rows = current.shape[1]
    length = green.shape[3]
    extent = length // 2
    planes = (green.shape[0] + 1) // 2
    strip_rows = extent // devices
    narrow = length // devices
    cell_count = strip_rows * planes * extent
    cos_table, sin_table = angle_tables(length, extent)
    is_live = voxel >= 0
    loaded = jnp.where(is_live, current, 0.0)
    send_values = jnp.zeros((devices, block_rows), jnp.float32).at[owner].set(loaded)
    send_places = jnp.full((devices, block_rows), -1, jnp.int32).at[owner].set(voxel)
    got_values, got_places = (
        lax.all_to_all(send_values, ("row", "col"), split_axis=0, concat_axis=0, tiled=True),
        lax.all_to_all(send_places, ("row", "col"), split_axis=0, concat_axis=0, tiled=True),
    )
    targets = jnp.where(got_places >= 0, got_places, cell_count).reshape(-1)
    source = (
        jnp.zeros((cell_count,), jnp.float32).at[targets].add(got_values.reshape(-1), mode="drop")
    )
    real_first, imag_first = forward_rows(
        source.reshape(strip_rows * planes, extent), cos_table, sin_table, length
    )
    spread = jnp.stack(
        [
            real_first.reshape(strip_rows, planes, length),
            imag_first.reshape(strip_rows, planes, length),
        ],
        axis=2,
    )
    pencil = lax.all_to_all(spread, ("row", "col"), split_axis=3, concat_axis=0, tiled=True)
    pencil = pencil.reshape(extent, planes * 2 * narrow)
    cosine_sum, sine_sum = forward_columns(pencil, cos_table, sin_table, length)
    cosine_sum = cosine_sum.reshape(planes, 2, narrow, length)
    sine_sum = sine_sum.reshape(planes, 2, narrow, length)
    spectral_real = cosine_sum[:, 0] + sine_sum[:, 1]
    spectral_imag = cosine_sum[:, 1] - sine_sum[:, 0]
    mixed_real = []
    mixed_imag = []
    for target in range(planes):
        total_real = jnp.zeros_like(spectral_real[0])
        total_imag = jnp.zeros_like(spectral_imag[0])
        for anchor in range(planes):
            kernel = green[target - anchor + planes - 1]
            total_real = (
                total_real + kernel[0] * spectral_real[anchor] - kernel[1] * spectral_imag[anchor]
            )
            total_imag = (
                total_imag + kernel[0] * spectral_imag[anchor] + kernel[1] * spectral_real[anchor]
            )
        mixed_real.append(total_real)
        mixed_imag.append(total_imag)
    mixed = jnp.stack([jnp.stack(mixed_real), jnp.stack(mixed_imag)], axis=1).reshape(
        planes * 2 * narrow, length
    )
    back_cos, back_sin = inverse_columns(mixed, cos_table, sin_table, length, extent)
    back_cos = back_cos.reshape(extent, planes, 2, narrow)
    back_sin = back_sin.reshape(extent, planes, 2, narrow)
    column = jnp.stack(
        [back_cos[:, :, 0] - back_sin[:, :, 1], back_sin[:, :, 0] + back_cos[:, :, 1]], axis=2
    )
    returned_rows = lax.all_to_all(column, ("row", "col"), split_axis=0, concat_axis=3, tiled=True)
    real_rows = returned_rows[:, :, 0].reshape(strip_rows * planes, length)
    imag_rows = returned_rows[:, :, 1].reshape(strip_rows * planes, length)
    volume = inverse_rows(real_rows, imag_rows, cos_table, sin_table, length, extent) * (
        1.0 / (length * length)
    )
    volume = volume.reshape(-1)
    picked = jnp.where(got_places >= 0, volume[jnp.clip(got_places, 0, cell_count - 1)], 0.0)
    returned = lax.all_to_all(picked, ("row", "col"), split_axis=0, concat_axis=0, tiled=True)
    coupled = returned[owner]
    rates = jnp.zeros_like(current)
    for species in range(resist.shape[0]):
        rates = jnp.where(material == species, resist[species], rates)
    return jnp.where(is_live, rates * current + coupled, 0.0)


def solution(mesh):
    in_specs = (
        P(("row", "col"), None),
        P(("row", "col")),
        P(("row", "col"), None),
        P(("row", "col"), None),
        P(),
        P(None, None, ("row", "col"), None),
    )
    out_specs = P(("row", "col"), None)
    return jax.shard_map(shards, mesh=mesh, in_specs=in_specs, out_specs=out_specs, check_vma=False)
```

profile of v0, /device:TPU:1, one launch (start us, length us, event | category | flops | bytes accessed | tf_op | source)
XLA Modules:
  0.0 1003.8 jit_solution(6045601371940378526)
XLA Ops:
  2.1 11.5 %all-to-all-start = ((s32[128,1,128]{2,1,0:T(1,128)}), s32[128,1,128]{2,1,0:T(1,128)S(1)}, u32[]{:S(2)}, u32[]{:S(2)}) async-start(s32[128,1,128]{2,1,0:T(1,128)} %bitcast.9), calls=%async_computation | async-start | bytes 131072 | tf_op jit(solution)/shard_map/all_to_all | solution.py:91
  13.6 121.8 %fusion.7 = f32[2048,4096]{1,0:T(8,128)} fusion(), kind=kLoop, calls=%fused_computation.15 | loop fusion | flops 117440512 | bytes 33554432 | tf_op jit(solution)/shard_map/cos | solution.py:15
  135.4 122.9 %fusion.6 = f32[2048,4096]{1,0:T(8,128)} fusion(), kind=kLoop, calls=%fused_computation.14 | loop fusion | flops 117440512 | bytes 33554432 | tf_op jit(solution)/shard_map/sin | solution.py:15
  259.6 9.8 all-to-all-start.1
  269.5 9.5 all-to-all-done.1
  278.9 86.1 %scatter_custom_fusion.2 = f32[65536]{0:T(1024)S(1)} fusion(s32[16384]{0:T(1024)S(1)} %bitcast.123, f32[16384]{0:T(1024)S(1)} %bitcast.122, f32[]{:T(128)} %constant.25.clone.1), kind=kCustom, calls=%fused_computation.248 | custom fusion | flops 16384 | bytes 262148 | tf_op jit(solution)/shard_map/scatter-add | solution.py:95
  388.5 16.9 %fusion.292 = f32[32,4096]{1,0:T(8,128)S(1)} fusion(f32[32,4096]{1,0:T(8,128)S(1)} %fusion.289, f32[32,2048]{1,0:T(8,128)S(1)} %reshape.147, f32[2048,4096]{1,0:T(8,128)} %fusion.7), kind=kOutput, calls=%fused_computation.198 | convolution fusion | flops 402653184 | bytes 4521984 | tf_op jit(solution)/shard_map/dot_general | solution.py:25
  415.1 7.0 copy.51
  460.1 7.0 copy.52
  467.1 11.8 %fusion.393 = f32[4096,2,2,16]{3,2,1,0:T(2,128)} fusion(f32[16,2,1,4096]{0,2,1,3:T(1,128)} %copy.52, f32[16,2,1,4096]{0,2,1,3:T(1,128)} %copy.51), kind=kLoop, calls=%fused_computation.281 | loop fusion | flops 262144 | bytes 2097152
  478.9 13.2 %reshape.210 = f32[128,1,2048]{2,1,0:T(1,128)S(1)} reshape(f32[4096,2,2,16]{3,2,1,0:T(2,128)} %fusion.393) | data formatting | bytes 2097152
  492.1 23.2 %all_to_all.63 = f32[128,1,2048]{2,1,0:T(1,128)S(1)} all-to-all(f32[128,1,2048]{2,1,0:T(1,128)S(1)} %reshape.210), channel_id=1, replica_groups=mesh['row'=8,'col'=16] {'row','col'}, dimensions={0} | all-to-all | bytes 2097152 | tf_op jit(solution)/shard_map/all_to_all | solution.py:107
  519.0 12.6 %reshape.211 = f32[4096,2,2,16]{3,2,1,0:T(2,128)} reshape(f32[128,2048]{1,0:T(8,128)S(1)} %reduce) | data formatting | bytes 2097152
  531.5 12.4 %copy.61 = f32[16,2,2,128,32]{4,3,0,2,1:T(8,128)} copy(f32[16,2,2,128,32]{0,2,1,4,3:T(2,128)} %bitcast.96) | data formatting | bytes 2097152 | tf_op jit(solution)/shard_map/all_to_all | solution.py:107
  543.9 7.4 copy.54
  672.7 6.6 fusion.58
  679.3 6.6 fusion.50
  685.9 6.8 fusion.42
  692.7 7.6 fusion.34
  700.3 6.6 fusion.18
  707.0 6.6 fusion.10
  713.6 6.8 fusion.145
  720.4 6.1 fusion.154
  726.5 7.0 fusion.166
  733.6 6.8 fusion.175
  745.0 6.5 reshape.212
  757.1 18.1 %all-to-all-done.3 = f32[128,1,2048]{2,1,0:T(1,128)S(1)} async-done(((f32[128,1,2048]{2,1,0:T(1,128)}), f32[128,1,2048]{2,1,0:T(1,128)S(1)}, u32[]{:S(2)}, u32[]{:S(2)}) %all-to-all-start.3) | async-done | bytes 1048608 | tf_op jit(solution)/shard_map/all_to_all | solution.py:138
  812.3 6.4 fusion.112
  836.8 6.2 fusion.24
  861.1 6.2 fusion.187
  891.5 90.5 %gather_fusion = f32[16384]{0:T(1024)S(1)} fusion(f32[65536]{0:T(1024)S(1)} %bitcast.93, s32[16384]{0:T(1024)S(1)} %fusion.368), kind=kCustom, calls=%fused_computation | custom fusion | bytes 196608 | tf_op jit(solution)/shard_map/gather | solution.py:145
  987.6 9.7 all-to-all-done.4
  (124 shorter events, 318.2 us)
Async XLA Ops:
  0.7 257.7 %copy-start.7 = (s32[32]{0:T(128)}, s32[32]{0:T(128)S(1)}, u32[]{:S(2)}) copy-start(s32[32]{0:T(128)S(1)} %compare_select_fusion.4) | copy-start | bytes 388
  2.1 257.5 %all-to-all-start = ((s32[128,1,128]{2,1,0:T(1,128)}), s32[128,1,128]{2,1,0:T(1,128)S(1)}, u32[]{:S(2)}, u32[]{:S(2)}) async-start(s32[128,1,128]{2,1,0:T(1,128)} %bitcast.9), calls=%async_computation | async-start | bytes 131072 | tf_op jit(solution)/shard_map/all_to_all | solution.py:91
  135.4 122.9 %copy-start.1 = (s32[32,128]{1,0:T(8,128)S(1)}, s32[32,128]{1,0:T(8,128)}, u32[]{:S(2)}) copy-start(s32[32,128]{1,0:T(8,128)} %param.8) | copy-start | bytes 49156
  135.4 122.9 %copy-start.3 = (f32[32,128]{1,0:T(8,128)S(1)}, f32[32,128]{1,0:T(8,128)}, u32[]{:S(2)}) copy-start(f32[32,128]{1,0:T(8,128)} %param.6) | copy-start | bytes 49156
  259.6 19.4 %all-to-all-start.1 = ((f32[128,1,128]{2,1,0:T(1,128)}), f32[128,1,128]{2,1,0:T(1,128)S(1)}, u32[]{:S(2)}, u32[]{:S(2)}) async-start(f32[128,1,128]{2,1,0:T(1,128)} %bitcast.12), calls=%async_computation.1 | async-start | bytes 131072 | tf_op jit(solution)/shard_map/all_to_all | solution.py:90
  599.9 37.6 %slice-start = ((s8[33554432]{0:T(1024)(128)(4,1)}), s8[4194304]{0:T(1024)(128)(4,1)S(1)}, s32[]{:S(2)}) async-start(s8[33554432]{0:T(1024)(128)(4,1)} %bitcast.94), calls=%async_computation.5 | async-start | bytes 8388608
  605.0 32.5 %slice-start.1 = ((s8[33554432]{0:T(1024)(128)(4,1)}), s8[4194304]{0:T(1024)(128)(4,1)S(1)}, s32[]{:S(2)}) async-start(s8[33554432]{0:T(1024)(128)(4,1)} %bitcast.94), calls=%async_computation.6 | async-start | bytes 8388608
  610.0 27.6 %slice-start.2 = ((s8[33554432]{0:T(1024)(128)(4,1)}), s8[4194304]{0:T(1024)(128)(4,1)S(1)}, s32[]{:S(2)}) async-start(s8[33554432]{0:T(1024)(128)(4,1)} %bitcast.94), calls=%async_computation.7 | async-start | bytes 8388608
  619.7 17.8 %slice-start.3 = ((s8[33554432]{0:T(1024)(128)(4,1)}), s8[4194304]{0:T(1024)(128)(4,1)S(1)}, s32[]{:S(2)}) async-start(s8[33554432]{0:T(1024)(128)(4,1)} %bitcast.94), calls=%async_computation.8 | async-start | bytes 8388608
  624.9 12.7 %slice-start.4 = ((s8[33554432]{0:T(1024)(128)(4,1)}), s8[4194304]{0:T(1024)(128)(4,1)S(1)}, s32[]{:S(2)}) async-start(s8[33554432]{0:T(1024)(128)(4,1)} %bitcast.94), calls=%async_computation.9 | async-start | bytes 8388608
  634.7 1.9 copy-start
  634.7 3.1 slice-start.5
  636.6 2.8 slice-start.6
  637.2 3.3 slice-start.7
  745.0 11.3 %copy-start.5 = (f32[8]{0:T(128)S(1)}, f32[8]{0:T(128)}, u32[]{:S(2)}) copy-start(f32[8]{0:T(128)} %param.10) | copy-start | bytes 100
  751.5 23.7 %all-to-all-start.3 = ((f32[128,1,2048]{2,1,0:T(1,128)}), f32[128,1,2048]{2,1,0:T(1,128)S(1)}, u32[]{:S(2)}, u32[]{:S(2)}) async-start(f32[128,1,2048]{2,1,0:T(1,128)} %reshape.212), calls=%async_computation.3 | async-start | bytes 2097152 | tf_op jit(solution)/shard_map/all_to_all | solution.py:138
  891.5 96.0 %copy-start.8 = (s32[32]{0:T(128)S(1)}, s32[32]{0:T(128)}, u32[]{:S(2)}) copy-start(s32[32]{0:T(128)} %copy-done.7) | copy-start | bytes 388
  891.5 106.3 %copy-start.2 = (s32[32,128]{1,0:T(8,128)S(1)}, s32[32,128]{1,0:T(8,128)}, u32[]{:S(2)}) copy-start(s32[32,128]{1,0:T(8,128)} %param.8) | copy-start | bytes 49156
  891.5 106.3 %copy-start.4 = (f32[32,128]{1,0:T(8,128)S(1)}, f32[32,128]{1,0:T(8,128)}, u32[]{:S(2)}) copy-start(f32[32,128]{1,0:T(8,128)} %param.6) | copy-start | bytes 49156
  891.5 106.3 %copy-start.6 = (s32[32,128]{1,0:T(8,128)S(1)}, s32[32,128]{1,0:T(8,128)}, u32[]{:S(2)}) copy-start(s32[32,128]{1,0:T(8,128)} %param.9) | copy-start | bytes 49156
  982.8 14.4 %all-to-all-start.4 = ((f32[128,1,128]{2,1,0:T(1,128)}), f32[128,1,128]{2,1,0:T(1,128)S(1)}, u32[]{:S(2)}, u32[]{:S(2)}) async-start(f32[128,1,128]{2,1,0:T(1,128)} %compare_select_fusion.2), calls=%async_computation.4 | async-start | bytes 131072 | tf_op jit(solution)/shard_map/all_to_all | solution.py:146
where the time goes:
time: 1010 us; the launch traced here: 1000 us
  matrix products  362 us (36%)
  other arithmetic  359 us (36%)
  local copies, waits for them, and re-layouts  190 us (19%)
  waiting for transfers between devices  37.3 us (4%)
  starting transfers between devices  30.7 us (3%)
  blocking collectives  23.2 us (2%)
    sin x1, other arithmetic, angle_tables(): return (jnp.cos(angles), jnp.sin(angles))  123 us
    cos x1, other arithmetic, angle_tables(): return (jnp.cos(angles), jnp.sin(angles))  122 us
    gather x1, local copies, waits for them, and re-layouts, shards(): volume[jnp.clip(got_places, 0, cell_count - 1)]  90.5 us
    scatter-add x1, other arithmetic, shards(): jnp.zeros((cell_count,), jnp.float32).at[targets]  86.1 us
    dot_general x8, matrix products, inverse_columns(): lax.dot_general(sine_part, section, contract, precision=highest)  54.8 us
    dot_general x8, matrix products, forward_rows(): real_parts.append(jnp.dot(matrix, cosine, precision=highest))  49.6 us
    dot_general x8, matrix products, inverse_rows(): lax.dot_general(real_part[:, offset:offset + block_cols], cosine, contrac...  48.8 us
    dot_general x8, matrix products, inverse_rows(): lax.dot_general(imag_part[:, offset:offset + block_cols], sine_part, cont...  48.3 us
  transfers between devices with their start and end apart: 4, of which 3 were waited for; matrix products, arithmetic and copies ran while one was open for 25% of the time, Pallas kernels for 0%

commit v1 on v0

v1 whole, which is shorter than its diff:
```python
import functools
import math

import jax
import jax.numpy as jnp
import ml_dtypes
import numpy as np
from jax import lax
from jax.experimental import pallas as pl
from jax.experimental.pallas import tpu as pltpu
from jax.sharding import PartitionSpec as P

F32 = jnp.float32
BF16 = jnp.bfloat16
LANES = 128


def halves(table):
    high = table.astype(ml_dtypes.bfloat16)
    low = (table - high.astype(np.float64)).astype(ml_dtypes.bfloat16)
    return high, low


def stacked(table, axis):
    high, low = halves(table)
    return np.concatenate([high, high, low], axis=axis)


def angles(left, right, length):
    return 2.0 * math.pi * (np.outer(left, right) % length) / length


@functools.lru_cache(maxsize=None)
def tables():
    out = {}
    j32, a16, n128, n64, a32 = (np.arange(n) for n in (32, 16, 128, 64, 32))
    theta = angles(j32, a16, 32)
    out["y_first"] = stacked(np.concatenate([np.cos(theta), -np.sin(theta)], axis=0), 1)
    theta = angles(j32, n128, 4096)
    out["y_turn"] = np.stack([np.cos(theta), -np.sin(theta)]).astype(np.float32)
    theta = angles(n128, n128, 128)
    cosine, sine = np.cos(theta), np.sin(theta)
    out["y_second"] = stacked(np.block([[cosine, -sine], [sine, cosine]]), 0)
    out["y_back"] = stacked(np.concatenate([cosine, sine], axis=1), 1)
    theta = np.tile(angles(n128, j32, 4096), (1, 4))
    sign = np.where(np.arange(128) < 64, -1.0, 1.0)
    out["y_unturn"] = np.stack([np.cos(theta), np.sin(theta) * sign]).astype(np.float32)
    theta = angles(j32, a16, 32)
    last = np.zeros((4, 2, 2, 32, 4, 2, 16))
    for x in range(4):
        for z in range(2):
            last[x, 0, z, :, x, z, :] = np.cos(theta)
            last[x, 1, z, :, x, z, :] = -np.sin(theta)
    out["y_last"] = stacked(last.reshape(512, 128), 0)
    first = []
    final = []
    for b in range(64):
        theta = angles(n64, 64 * a32 + b, 4096)
        first.append(stacked(np.concatenate([np.cos(theta), np.sin(theta)], axis=1), 1))
        final.append(stacked(np.concatenate([np.cos(theta.T), np.sin(theta.T)], axis=1), 1))
    out["x_first"] = np.concatenate(first, axis=0)
    out["x_final"] = np.concatenate(final, axis=0)
    theta = angles(n64, n64, 64)
    out["x_mid"] = stacked(np.concatenate([np.cos(theta), np.sin(theta)], axis=1), 1)
    return out


def split(value):
    high = value.astype(BF16)
    return high, (value - high.astype(F32)).astype(BF16)


def lane_sign(shape, low, high):
    lane = lax.broadcasted_iota(jnp.int32, shape, 1)
    return jnp.where(lane % LANES < LANES // 2, low, high).astype(F32)


def paired(value, low):
    swapped = pltpu.roll(value, LANES // 2, 1) * lane_sign(value.shape, low, -low)
    high, rest = split(value)
    high_s, rest_s = split(swapped)
    return jnp.concatenate([high, high_s, rest, rest_s, high, high_s], axis=0)


def dot(left, right, dims=(((1,), (0,)), ((), ()))):
    return lax.dot_general(left, right, dims, preferred_element_type=F32)


def pack_kernel(owner_ref, current_ref, voxel_ref, values_ref, places_ref):
    blocks = current_ref.shape[0]
    voxel = voxel_ref[...]
    loaded = jnp.where(voxel >= 0, current_ref[...], 0.0)
    values = jnp.zeros(values_ref.shape, F32)
    places = jnp.full(places_ref.shape, -1, jnp.int32)
    ids = lax.broadcasted_iota(jnp.int32, values.shape, 0)
    for block in range(blocks):
        mine = ids == owner_ref[block]
        values = jnp.where(mine, loaded[block : block + 1], values)
        places = jnp.where(mine, voxel[block : block + 1], places)
    values_ref[...] = values
    places_ref[...] = places


def one_hot(index, count):
    ids = lax.broadcasted_iota(jnp.int32, (count, index.shape[1]), 0)
    return jnp.where(ids == index, 1.0, 0.0).astype(BF16)


def fill_kernel(values_ref, places_ref, first_ref, turn_ref, second_ref, send_ref, slab_ref, left_ref):
    slab_ref[...] = jnp.zeros_like(slab_ref)

    @pl.loop(0, 16)
    def _(step):
        rows = pl.ds(pl.multiple_of(step * 8, 8), 8)
        places = places_ref[rows, :]
        values = values_ref[rows, :]
        high = values.astype(BF16).astype(F32)
        low = values - high
        tops, spots = [], []
        ids = lax.broadcasted_iota(jnp.int32, (LANES, LANES), 0)
        for s in range(8):
            place = places[s : s + 1]
            tops.append(one_hot(place >> 7, 512))
            hit = ids == (place & 127)
            spots.append(
                jnp.concatenate(
                    [
                        jnp.where(hit, high[s : s + 1], 0.0).astype(BF16),
                        jnp.where(hit, low[s : s + 1], 0.0).astype(BF16),
                    ],
                    axis=0,
                )
            )
        top = jnp.concatenate(tops, axis=1)
        spot = jnp.concatenate(spots, axis=1)
        slab_ref[...] += dot(top, spot, (((1,), (1,)), ((), ())))

    slab = slab_ref[:, :LANES] + slab_ref[:, LANES:]
    wide = jnp.concatenate([slab[16 * i : 16 * i + 16] for i in range(32)], axis=1)
    high, low = split(wide)
    begun = dot(first_ref[...], jnp.concatenate([high, low, high], axis=0))
    turn_re, turn_im = turn_ref[0], turn_ref[1]
    for i in range(32):
        re = begun[:32, LANES * i : LANES * i + LANES]
        im = begun[32:, LANES * i : LANES * i + LANES]
        both = jnp.concatenate(
            [re * turn_re - im * turn_im, re * turn_im + im * turn_re], axis=1
        )
        high, low = split(both)
        left_ref[32 * i : 32 * i + 32, :] = jnp.concatenate([high, low, high], axis=1)
    spectra = dot(left_ref[...], second_ref[...])
    for x in range(16):
        part = spectra[64 * x : 64 * x + 64]
        part = jnp.concatenate([part[:, :LANES], part[:, LANES:]], axis=0)
        send_ref[pl.ds(x, LANES, stride=16), :] = part.T


def mix_kernel(pencil_ref, green_ref, first_ref, mid_ref, final_ref, send_ref, half_ref, back_ref, coef_ref):
    @pl.loop(0, 32)
    def _(tile):
        cols = pl.ds(pl.multiple_of(tile * LANES, LANES), LANES)
        rows = pl.ds(pl.multiple_of(tile * LANES, LANES), LANES)
        re = [green_ref[o, 0, :, cols] for o in range(3)]
        im = [green_ref[o, 1, :, cols] for o in range(3)]
        arranged = [
            [re[1], re[1], re[1], re[1]],
            [re[0], -im[2], re[0], im[2]],
            [-im[1], -im[1], im[1], im[1]],
            [-im[0], re[2], im[0], re[2]],
        ]
        for g in range(4):
            coef_ref[g, rows, :] = jnp.concatenate(arranged[g], axis=0).T

    for b in range(64):
        rows = pencil_ref[pl.ds(b, 32, stride=64), :]
        begun = dot(first_ref[64 * b : 64 * b + 64, :], paired(rows, 1.0))
        half_ref[pl.ds(b, 64, stride=64), :] = begun

    mid = mid_ref[...]
    for k in range(64):
        spectrum = dot(mid, paired(half_ref[64 * k : 64 * k + 64, :], 1.0))
        mixed = jnp.zeros_like(spectrum)
        for g in range(4):
            turned = spectrum if g == 0 else pltpu.roll(spectrum, LANES - 32 * g, 1)
            mixed = mixed + coef_ref[g, pl.ds(k, 64, stride=64), :] * turned
        back_ref[pl.ds(k, 64, stride=64), :] = dot(mid, paired(mixed, -1.0))

    for b in range(64):
        send_ref[pl.ds(b, 32, stride=64), :] = dot(
            final_ref[32 * b : 32 * b + 32, :], paired(back_ref[64 * b : 64 * b + 64, :], -1.0)
        )


def read_kernel(field_ref, places_ref, back_ref, unturn_ref, last_ref, picked_ref):
    back = back_ref[...]
    cosine, sine = unturn_ref[0], unturn_ref[1]
    pieces = []
    for quad in range(4):
        turned = []
        for i in range(4):
            rows = field_ref[pl.ds(4 * quad + i, LANES, stride=16), :]
            piece = dot(back, paired(rows, -1.0))
            turned.append(piece * cosine + pltpu.roll(piece, LANES // 2, 1) * sine)
        high, low = split(jnp.concatenate(turned, axis=1))
        pieces.append(dot(jnp.concatenate([high, low, high], axis=1), last_ref[...]))
    high, low = split(jnp.concatenate(pieces, axis=1) * (1.0 / 16777216.0))
    volume = jnp.concatenate([high, low], axis=0)
    ids = lax.broadcasted_iota(jnp.int32, (LANES, LANES), 0)

    @pl.loop(0, 16)
    def _(step):
        rows = pl.ds(pl.multiple_of(step * 8, 8), 8)
        places = places_ref[rows, :]
        top = jnp.concatenate([one_hot(places[s : s + 1] >> 7, 512) for s in range(8)], axis=1)
        found = dot(volume, top)
        lines = []
        for s in range(8):
            line = found[:LANES, LANES * s : LANES * s + LANES] + found[LANES:, LANES * s : LANES * s + LANES]
            line = jnp.where(ids == (places[s : s + 1] & 127), line, 0.0)
            lines.append(jnp.sum(line, axis=0, keepdims=True))
        picked_ref[rows, :] = jnp.concatenate(lines, axis=0)


def finish_kernel(owner_ref, resist_ref, returned_ref, current_ref, voxel_ref, material_ref, out_ref):
    blocks = current_ref.shape[0]
    material = material_ref[...]
    rates = jnp.zeros(current_ref.shape, F32)
    for kind in range(8):
        rates = jnp.where(material == kind, resist_ref[kind], rates)
    coupled = jnp.concatenate(
        [returned_ref[pl.ds(owner_ref[b], 1), :] for b in range(blocks)], axis=0
    )
    out_ref[...] = jnp.where(voxel_ref[...] >= 0, rates * current_ref[...] + coupled, 0.0)


VM = pl.BlockSpec(memory_space=pltpu.VMEM)
SM = pl.BlockSpec(memory_space=pltpu.SMEM)
PARAMS = pltpu.CompilerParams(vmem_limit_bytes=56 * 1024 * 1024)


def call(kernel, out, ins, scratch=()):
    return pl.pallas_call(
        kernel,
        out_shape=out,
        in_specs=ins,
        out_specs=jax.tree.map(lambda _: VM, out),
        scratch_shapes=list(scratch),
        compiler_params=PARAMS,
    )


def shards(current, owner, voxel, material, resist, green):
    shape = jax.ShapeDtypeStruct
    t = tables()
    axes = ("row", "col")
    swap = functools.partial(lax.all_to_all, axis_name=axes, split_axis=0, concat_axis=0, tiled=True)
    values, places = call(
        pack_kernel, (shape((128, 128), F32), shape((128, 128), jnp.int32)), [SM, VM, VM]
    )(owner, current, voxel)
    values, places = swap(values), swap(places)
    spread = call(
        fill_kernel,
        shape((2048, LANES), F32),
        [VM] * 5,
        [pltpu.VMEM((512, 256), F32), pltpu.VMEM((1024, 768), BF16)],
    )(values, places, t["y_first"], t["y_turn"], t["y_second"])
    pencil = swap(spread)
    field = call(
        mix_kernel,
        shape((2048, LANES), F32),
        [VM] * 5,
        [
            pltpu.VMEM((4096, LANES), F32),
            pltpu.VMEM((4096, LANES), F32),
            pltpu.VMEM((4, 4096, LANES), F32),
        ],
    )(pencil, green, t["x_first"], t["x_mid"], t["x_final"])
    field = swap(field)
    picked = call(read_kernel, shape((128, 128), F32), [VM] * 5)(
        field, places, t["y_back"], t["y_unturn"], t["y_last"]
    )
    returned = swap(picked)
    return call(finish_kernel, shape(current.shape, F32), [SM, SM, VM, VM, VM, VM])(
        owner, resist, returned, current, voxel, material
    )


def solution(mesh):
    in_specs = (
        P(("row", "col"), None),
        P(("row", "col")),
        P(("row", "col"), None),
        P(("row", "col"), None),
        P(),
        P(None, None, ("row", "col"), None),
    )
    out_specs = P(("row", "col"), None)
    return jax.shard_map(shards, mesh=mesh, in_specs=in_specs, out_specs=out_specs, check_vma=False)
```

time: 1010 us -> 164 us (0.16)
  matrix products: 362 us -> 0 us
  other arithmetic: 359 us -> 0 us
  local copies, waits for them, and re-layouts: 190 us -> 0 us
  blocking collectives: 23.2 us -> 101 us
  Pallas kernels: 0 us -> 62.4 us
  waiting for transfers between devices: 37.3 us -> 0 us
  starting transfers between devices: 30.7 us -> 0 us
    dot_general x64 -> x0, matrix products: 362 us -> none  [the longest x8 54.8 us: inverse_columns(): lax.dot_general(sine_part, section, contract, precision=highest)]
    sin x1 -> x0, other arithmetic: 123 us -> none  [angle_tables(): return (jnp.cos(angles), jnp.sin(angles))]
    cos x1 -> x0, other arithmetic: 122 us -> none  [angle_tables(): return (jnp.cos(angles), jnp.sin(angles))]
    gather x2 -> x0, local copies, waits for them, and re-layouts: 91.1 us -> none  [the longest x1 90.5 us: shards(): volume[jnp.clip(got_places, 0, cell_count - 1)]]
    scatter-add x1 -> x0, other arithmetic: 86.1 us -> none  [shards(): jnp.zeros((cell_count,), jnp.float32).at[targets]]
    all_to_all x1 -> x5, blocking collectives: 23.2 us -> 101 us  [the longest x2 36.8 us: shards(): values, places = (swap(values), swap(places))]
    pallas_call x0 -> x5, Pallas kernels: none -> 62.4 us  [the longest x1 36.1 us: shards(): call(mix_kernel, shape((2048, LANES), F32), [VM] * 5, [pltpu.VMEM((4096,...]
    unnamed x39 -> x0, local copies, waits for them, and re-layouts: 41.7 us -> none
  transfers between devices with their start and end apart: 4 -> 0, of which waited for: 3 -> 0; matrix products, arithmetic and copies ran while one was open for 25% -> 0% of each run, Pallas kernels for 0% -> 0%
where the time goes in v1:
time: 164 us; the launch traced here: 163 us
  blocking collectives  101 us (62%)
  Pallas kernels  62.4 us (38%)
    all_to_all x2, blocking collectives, shards(): values, places = (swap(values), swap(places))  36.8 us
    pallas_call x1, Pallas kernels, shards(): call(mix_kernel, shape((2048, LANES), F32), [VM] * 5, [pltpu.VMEM((4096,...  36.1 us
    all_to_all x1, blocking collectives, shards(): field = swap(field)  24.6 us
    all_to_all x1, blocking collectives, shards(): pencil = swap(spread)  24.2 us
    all_to_all x1, blocking collectives, shards(): returned = swap(picked)  15.5 us
    pallas_call x1, Pallas kernels, shards(): call(read_kernel, shape((128, 128), F32), [VM] * 5)  11.7 us
    pallas_call x1, Pallas kernels, shards(): call(fill_kernel, shape((2048, LANES), F32), [VM] * 5, [pltpu.VMEM((512,...  11.3 us

profile of v1, /device:TPU:1, one launch (start us, length us, event | category | flops | bytes accessed | tf_op | source)
XLA Modules:
  0.0 163.5 jit_solution(2443163891507339182)
XLA Ops:
  0.0 1.8 %shard_map.145 = (f32[128,128]{1,0:T(8,128)}, s32[128,128]{1,0:T(8,128)}) custom-call(s32[32]{0:T(128)} %owner_ref.3, f32[32,128]{1,0:T(8,128)} %current_ref.3, s32[32,128]{1,0:T(8,128)} %voxel_ref.3), custom_call_target="tpu_custom_call" | custom-call | tf_op jit(solution)/shard_map/pallas_call | solution.py:257
  1.8 21.6 %all_to_all.55 = s32[128,1,128]{2,1,0:T(1,128)} all-to-all(s32[128,1,128]{2,1,0:T(1,128)} %bitcast.26), channel_id=1, replica_groups=mesh['row'=8,'col'=16] {'row','col'}, dimensions={0} | all-to-all | bytes 131072 | tf_op jit(solution)/shard_map/all_to_all | solution.py:260
  23.4 15.3 %all_to_all.56 = f32[128,1,128]{2,1,0:T(1,128)} all-to-all(f32[128,1,128]{2,1,0:T(1,128)} %bitcast.25), channel_id=1, replica_groups=mesh['row'=8,'col'=16] {'row','col'}, dimensions={0} | all-to-all | bytes 131072 | tf_op jit(solution)/shard_map/all_to_all | solution.py:260
  38.6 11.3 %shard_map.146 = f32[2048,128]{1,0:T(8,128)} custom-call(f32[128,128]{1,0:T(8,128)} %bitcast.22, s32[128,128]{1,0:T(8,128)} %bitcast.20, bf16[64,48]{1,0:T(8,128)(2,1)} %constant.18.clone.first_ref, f32[2,32,128]{2,1,0:T(8,128)} %constant.19.clone.turn_ref, bf16[768,256]{1,0:T(8,128)(2,1)} %constant.20.clone.second_ref), custom_call_target="tpu_custom_call" | custom-call | tf_op jit(solution)/shard_map/pallas_call | solution.py:261
  49.9 24.2 %all_to_all.57 = f32[128,16,128]{2,1,0:T(8,128)} all-to-all(f32[128,16,128]{2,1,0:T(8,128)} %bitcast.19), channel_id=1, replica_groups=mesh['row'=8,'col'=16] {'row','col'}, dimensions={0} | all-to-all | bytes 2097152 | tf_op jit(solution)/shard_map/all_to_all | solution.py:267
  74.1 36.1 %shard_map.147 = f32[2048,128]{1,0:T(8,128)} custom-call(f32[2048,128]{1,0:T(8,128)} %bitcast.16, f32[3,2,32,4096]{3,2,1,0:T(8,128)} %green_ref.1, bf16[4096,192]{1,0:T(8,128)(2,1)} %constant.21.clone.first_ref, bf16[64,384]{1,0:T(8,128)(2,1)} %constant.22.clone.mid_ref, bf16[2048,384]{1,0:T(8,128)(2,1)} %constant.23.clone.final_ref), custom_call_target="tpu_custom_call" | custom-call | tf_op jit(solution)/shard_map/pallas_call | solution.py:268
  110.2 24.6 %all_to_all.58 = f32[128,16,128]{2,1,0:T(8,128)} all-to-all(f32[128,16,128]{2,1,0:T(8,128)} %bitcast.17), channel_id=1, replica_groups=mesh['row'=8,'col'=16] {'row','col'}, dimensions={0} | all-to-all | bytes 2097152 | tf_op jit(solution)/shard_map/all_to_all | solution.py:278
  134.8 11.7 %shard_map.148 = f32[128,128]{1,0:T(8,128)} custom-call(f32[2048,128]{1,0:T(8,128)} %bitcast.18, s32[128,128]{1,0:T(8,128)} %bitcast.21, bf16[128,768]{1,0:T(8,128)(2,1)} %constant.24.clone.back_ref, f32[2,128,128]{2,1,0:T(8,128)} %constant.25.clone.unturn_ref, bf16[1536,128]{1,0:T(8,128)(2,1)} %constant.26.clone.last_ref), custom_call_target="tpu_custom_call" | custom-call | tf_op jit(solution)/shard_map/pallas_call | solution.py:279
  146.5 15.5 %all_to_all.59 = f32[128,1,128]{2,1,0:T(1,128)} all-to-all(f32[128,1,128]{2,1,0:T(1,128)} %bitcast.24), channel_id=1, replica_groups=mesh['row'=8,'col'=16] {'row','col'}, dimensions={0} | all-to-all | bytes 131072 | tf_op jit(solution)/shard_map/all_to_all | solution.py:282
  162.0 1.5 shard_map.149

commit v2 on v1

v2 whole, which is shorter than its diff:
```python
import functools
import math

import jax
import jax.numpy as jnp
import ml_dtypes
import numpy as np
from jax import lax
from jax.experimental import pallas as pl
from jax.experimental.pallas import tpu as pltpu
from jax.sharding import PartitionSpec as P

F32 = jnp.float32
BF16 = jnp.bfloat16
LANES = 128


def halves(table):
    high = table.astype(ml_dtypes.bfloat16)
    low = (table - high.astype(np.float64)).astype(ml_dtypes.bfloat16)
    return high, low


def stacked(table, axis):
    high, low = halves(table)
    return np.concatenate([high, high, low], axis=axis)


def angles(left, right, length):
    return 2.0 * math.pi * (np.outer(left, right) % length) / length


@functools.lru_cache(maxsize=None)
def tables():
    out = {}
    j32, a16, n128, n64, a32 = (np.arange(n) for n in (32, 16, 128, 64, 32))
    theta = angles(j32, a16, 32)
    out["y_first"] = stacked(np.concatenate([np.cos(theta), -np.sin(theta)], axis=0), 1)
    theta = angles(j32, n128, 4096)
    out["y_turn"] = np.stack([np.cos(theta), -np.sin(theta)]).astype(np.float32)
    theta = angles(n128, n128, 128)
    cosine, sine = np.cos(theta), np.sin(theta)
    out["y_second"] = stacked(np.block([[cosine, -sine], [sine, cosine]]), 0)
    out["y_back"] = stacked(np.concatenate([cosine, sine], axis=0), 1)
    theta = np.tile(angles(n128, j32, 4096), (1, 4))
    sign = np.where(np.arange(128) < 64, -1.0, 1.0)
    out["y_unturn"] = np.stack([np.cos(theta), np.sin(theta) * sign]).astype(np.float32)
    theta = angles(j32, a16, 32)
    last = np.zeros((4, 2, 2, 32, 4, 2, 16))
    for x in range(4):
        for z in range(2):
            last[x, 0, z, :, x, z, :] = np.cos(theta)
            last[x, 1, z, :, x, z, :] = -np.sin(theta)
    out["y_last"] = stacked(last.reshape(512, 128), 0)
    first = []
    final = []
    for b in range(64):
        theta = angles(n64, 64 * a32 + b, 4096)
        first.append(stacked(np.concatenate([np.cos(theta), np.sin(theta)], axis=0), 1))
        final.append(stacked(np.concatenate([np.cos(theta.T), np.sin(theta.T)], axis=0), 1))
    out["x_first"] = np.concatenate(first, axis=0)
    out["x_final"] = np.concatenate(final, axis=0)
    theta = angles(n64, n64, 64)
    out["x_mid"] = stacked(np.concatenate([np.cos(theta), np.sin(theta)], axis=0), 1)
    return out


def split(value):
    high = value.astype(BF16)
    return high, (value - high.astype(F32)).astype(BF16)


MESH = pl.DeviceIdType.MESH
ROWS, COLS, EDGE = 8, 16, 4
NAMES = (
    "y_first", "y_turn", "y_second", "x_first", "x_mid", "x_final", "y_back", "y_unturn", "y_last",
)


def dot(left, right, dims=(((1,), (0,)), ((), ()))):
    return lax.dot_general(left, right, dims, preferred_element_type=F32)


def triple(value):
    high, low = split(value)
    return jnp.concatenate([high, low, high], axis=0)


def combine(product, place, low):
    count = product.shape[0] // 2
    cosine = product[:count, LANES * place : LANES * place + LANES]
    sine = product[count:, LANES * place : LANES * place + LANES]
    lane = lax.broadcasted_iota(jnp.int32, (count, LANES), 1)
    sign = jnp.where(lane < LANES // 2, low, -low).astype(F32)
    return cosine + pltpu.roll(sine, LANES // 2, 1) * sign


def aligned(value, step):
    return pl.multiple_of(value * step, step)


def kernel(
    owner_ref, resist_ref, current_ref, voxel_ref, material_ref, green_hbm, *rest
):
    count = len(NAMES)
    tables_hbm, out_ref = rest[:count], rest[count]
    (
        green_ref, route_out, route_in, spread_ref, pencil_ref, field_out, field_in, picked_ref, returned_ref,
        slab_ref, top_ref, left_ref, half_ref, back_ref, coef_ref,
    ) = rest[count + 1 : count + 16]
    held = rest[count + 16 : 2 * count + 16]
    load_sems, send_sems, route_sems, pencil_sems, field_sem, return_sem, spread_gate = rest[2 * count + 16 :]
    first_y, turn_ref, second_y, first_x, mid_x, final_x, back_y, unturn_ref, last_y = held

    row, col = lax.axis_index("row"), lax.axis_index("col")
    me = row * COLS + col
    high_col, low_col = col // EDGE, col % EDGE

    barrier = pltpu.get_barrier_semaphore()
    for k in range(1, ROWS):
        pl.semaphore_signal(barrier, inc=1, device_id=((row + k) % ROWS, col), device_id_type=MESH)
    for k in range(1, COLS):
        pl.semaphore_signal(barrier, inc=1, device_id=(row, (col + k) % COLS), device_id_type=MESH)

    loads = [pltpu.make_async_copy(green_hbm, green_ref, load_sems.at[count])]
    loads += [pltpu.make_async_copy(tables_hbm[i], held[i], load_sems.at[i]) for i in range(count)]
    for load in loads:
        load.start()

    voxel = voxel_ref[...]
    live = voxel >= 0
    loaded = jnp.where(live, current_ref[...], 0.0)
    cells = voxel.astype(F32)
    values = jnp.zeros((ROWS * COLS, LANES), F32)
    places = jnp.full((ROWS * COLS, LANES), -1.0, F32)
    ids = lax.broadcasted_iota(jnp.int32, values.shape, 0)
    for block in range(current_ref.shape[0]):
        mine = ids == owner_ref[block]
        values = jnp.where(mine, loaded[block : block + 1], values)
        places = jnp.where(mine, cells[block : block + 1], places)
    route_out[pl.ds(0, ROWS * COLS, stride=2), :] = values
    route_out[pl.ds(1, ROWS * COLS, stride=2), :] = places
    slab_ref[...] = jnp.zeros_like(slab_ref)

    pl.semaphore_wait(barrier, ROWS + COLS - 2)
    for k in range(1, COLS):
        pl.semaphore_signal(spread_gate, inc=1, device_id=(row, (col + k) % COLS), device_id_type=MESH)
    pl.semaphore_wait(spread_gate, COLS - 1)

    def remote(source, target, size, device, send_sem, recv_sem):
        index = device[0] * COLS + device[1]
        return pltpu.make_async_remote_copy(
            source.at[pl.ds(index * size, size)],
            target.at[pl.ds(me * size, size)],
            send_sem,
            recv_sem,
            device_id=device,
            device_id_type=MESH,
        )

    def local(source, target, size, recv_sem):
        mine = pl.ds(me * size, size)
        return pltpu.make_async_copy(source.at[mine], target.at[mine], recv_sem)

    local(route_out, route_in, 2, route_sems.at[0]).start()

    @pl.loop(1, ROWS * COLS)
    def _(k):
        device = ((row + k // COLS) % ROWS, (col + k % COLS) % COLS)
        remote(route_out, route_in, 2, device, send_sems.at[0], route_sems.at[k // COLS]).start()

    side = lax.broadcasted_iota(jnp.int32, (256, LANES), 0).astype(F32).astype(BF16)
    one, zero = jnp.ones((256, LANES), BF16), jnp.zeros((256, LANES), BF16)

    def arrived(step):
        block = route_in[pl.ds(aligned((row - step + ROWS) % ROWS, 2 * COLS), 2 * COLS), :]
        place = block.astype(jnp.int32)
        top = jnp.where(place < 0, -1, (place >> 7) & 255).astype(F32).astype(BF16)
        spot = (((place >> 15) & 1) * LANES + (place & 127)).astype(F32).astype(BF16)
        return block, top, spot

    @pl.loop(0, ROWS)
    def _(step):
        pltpu.make_async_copy(
            route_in.at[pl.ds(0, 2 * COLS)], route_in.at[pl.ds(0, 2 * COLS)], route_sems.at[step]
        ).wait()
        block, top, spot = arrived(step)
        high, low = split(block)
        spots = []
        for s in range(COLS):
            top_ref[step, :, LANES * s : LANES * s + LANES] = jnp.where(
                side == top[2 * s + 1 : 2 * s + 2], one, zero
            )
            hit = side == spot[2 * s + 1 : 2 * s + 2]
            spots.append(
                jnp.concatenate(
                    [
                        jnp.where(hit, high[2 * s : 2 * s + 1], zero),
                        jnp.where(hit, low[2 * s : 2 * s + 1], zero),
                    ],
                    axis=0,
                )
            )
        slab_ref[...] += dot(jnp.concatenate(spots, axis=1), top_ref[step], (((1,), (1,)), ((), ())))

    for load in loads[1:]:
        load.wait()
    slab = (slab_ref[:256, :] + slab_ref[256:, :]).T
    wide = jnp.concatenate(
        [
            slab[16 * (i % 16) : 16 * (i % 16) + 16, LANES * (i // 16) : LANES * (i // 16) + LANES]
            for i in range(32)
        ],
        axis=1,
    )
    begun = dot(first_y[...], triple(wide))
    turn_re, turn_im = turn_ref[0], turn_ref[1]
    for i in range(32):
        re = begun[:32, LANES * i : LANES * i + LANES]
        im = begun[32:, LANES * i : LANES * i + LANES]
        both = jnp.concatenate([re * turn_re - im * turn_im, re * turn_im + im * turn_re], axis=1)
        high, low = split(both)
        left_ref[32 * i : 32 * i + 32, :] = jnp.concatenate([high, low, high], axis=1)
    spectra = dot(left_ref[...], second_y[...])
    for x in range(16):
        part = spectra[64 * x : 64 * x + 64]
        part = jnp.concatenate([part[:, :LANES], part[:, LANES:]], axis=0)
        spread_ref[pl.ds(x, LANES, stride=16), :] = part.T

    local(spread_ref, pencil_ref, 16, pencil_sems.at[low_col]).start()

    @pl.loop(1, ROWS * COLS)
    def _(k):
        turn = k // (ROWS * EDGE)
        device = (
            (row + (k // EDGE) % ROWS) % ROWS,
            ((high_col + k % EDGE) % EDGE) * EDGE + (low_col + turn) % EDGE,
        )
        remote(spread_ref, pencil_ref, 16, device, send_sems.at[1], pencil_sems.at[low_col]).start()

    loads[0].wait()

    @pl.loop(0, 32)
    def _(tile):
        cols = pl.ds(aligned(tile, LANES), LANES)
        re = [green_ref[o, 0, :, cols] for o in range(3)]
        im = [green_ref[o, 1, :, cols] for o in range(3)]
        arranged = [
            [re[1], re[1], re[1], re[1]],
            [re[0], -im[2], re[0], im[2]],
            [-im[1], -im[1], im[1], im[1]],
            [-im[0], re[2], im[0], re[2]],
        ]
        for g in range(4):
            turned = jnp.concatenate(arranged[g], axis=0).T
            coef_ref[g, pl.ds(2 * tile, 64, stride=64), :] = turned[:64]
            coef_ref[g, pl.ds(2 * tile + 1, 64, stride=64), :] = turned[64:]

    @pl.loop(0, EDGE)
    def _(turn):
        group = (low_col - turn + EDGE) % EDGE
        quarter = pl.ds(0, ROWS * EDGE * 16)
        pltpu.make_async_copy(pencil_ref.at[quarter], pencil_ref.at[quarter], pencil_sems.at[group]).wait()
        for i in range(16):
            b = group * 16 + i
            rows = pencil_ref[pl.ds(b, 32, stride=64), :]
            product = dot(first_x[pl.ds(aligned(b, 128), 128), :], triple(rows))
            half_ref[pl.ds(b, 64, stride=64), :] = combine(product, 0, 1.0)

    mid = mid_x[...]
    for start in range(0, 64, 8):
        ks = range(start, start + 8)
        product = dot(
            mid, jnp.concatenate([triple(half_ref[64 * k : 64 * k + 64, :]) for k in ks], axis=1)
        )
        mixed = []
        for i, k in enumerate(ks):
            spectrum = combine(product, i, 1.0)
            total = coef_ref[0, 64 * k : 64 * k + 64, :] * spectrum
            for g in range(1, 4):
                total = total + coef_ref[g, 64 * k : 64 * k + 64, :] * pltpu.roll(spectrum, LANES - 32 * g, 1)
            mixed.append(triple(total))
        product = dot(mid, jnp.concatenate(mixed, axis=1))
        for i, k in enumerate(ks):
            back_ref[pl.ds(k, 64, stride=64), :] = combine(product, i, -1.0)

    @pl.loop(0, EDGE)
    def _(turn):
        group = (low_col + turn) % EDGE
        for i in range(16):
            b = group * 16 + i
            rows = back_ref[pl.ds(aligned(b, 64), 64), :]
            product = dot(final_x[pl.ds(aligned(b, 64), 64), :], triple(rows))
            field_out[pl.ds(b, 32, stride=64), :] = combine(product, 0, -1.0)

        @pl.when(turn == 0)
        def _():
            local(field_out, field_in, 16, field_sem).start()

        @pl.loop(jnp.where(turn == 0, 1, 0), ROWS * EDGE)
        def _(k):
            device = ((row + k // EDGE) % ROWS, ((high_col + k % EDGE) % EDGE) * EDGE + group)
            remote(field_out, field_in, 16, device, send_sems.at[2], field_sem).start()

    pltpu.make_async_copy(field_in, field_in, field_sem).wait()

    back = back_y[...]
    cosine, sine = unturn_ref[0], unturn_ref[1]
    pieces = []
    for quad in range(4):
        product = dot(
            back,
            jnp.concatenate(
                [triple(field_in[pl.ds(4 * quad + i, LANES, stride=16), :]) for i in range(4)], axis=1
            ),
        )
        turned = []
        for i in range(4):
            piece = combine(product, i, -1.0)
            turned.append(piece * cosine + pltpu.roll(piece, LANES // 2, 1) * sine)
        high, low = split(jnp.concatenate(turned, axis=1))
        pieces.append(dot(jnp.concatenate([high, low, high], axis=1), last_y[...]))
    volume = jnp.concatenate(
        [jnp.concatenate(pieces[:2], axis=1), jnp.concatenate(pieces[2:], axis=1)], axis=0
    ) * (1.0 / 16777216.0)
    volume = jnp.concatenate(split(volume), axis=0)

    spots = lax.broadcasted_iota(jnp.int32, (256, LANES), 0)

    @pl.loop(0, ROWS)
    def _(step):
        base = (row - step + ROWS) % ROWS
        place = route_in[pl.ds(aligned(base, 2 * COLS), 2 * COLS), :].astype(jnp.int32)
        spot = ((place >> 15) & 1) * LANES + (place & 127)
        found = dot(volume, top_ref[step])
        lines = []
        for s in range(COLS):
            line = found[:256, LANES * s : LANES * s + LANES] + found[256:, LANES * s : LANES * s + LANES]
            line = jnp.where(spots == spot[2 * s + 1 : 2 * s + 2], line, 0.0)
            lines.append(jnp.sum(line, axis=0, keepdims=True))
        picked_ref[pl.ds(aligned(base, COLS), COLS), :] = jnp.concatenate(lines, axis=0)

        @pl.when(step == 0)
        def _():
            local(picked_ref, returned_ref, 1, return_sem).start()

        @pl.loop(jnp.where(step == 0, 1, 0), COLS)
        def _(k):
            device = (base, (col + k) % COLS)
            remote(picked_ref, returned_ref, 1, device, send_sems.at[3], return_sem).start()

    rates = jnp.zeros(current_ref.shape, F32)
    for kind in range(8):
        rates = jnp.where(material_ref[...] == kind, resist_ref[kind], rates)
    own = rates * current_ref[...]
    pltpu.make_async_copy(returned_ref, returned_ref, return_sem).wait()
    coupled = jnp.concatenate(
        [returned_ref[pl.ds(owner_ref[b], 1), :] for b in range(current_ref.shape[0])], axis=0
    )
    out_ref[...] = jnp.where(live, own + coupled, 0.0)
    for i, (ref, size) in enumerate(((route_out, 2), (spread_ref, 16), (field_out, 16), (picked_ref, 1))):
        sent = ref.at[pl.ds(0, (ROWS * COLS - 1) * size)]
        pltpu.make_async_copy(sent, sent, send_sems.at[i]).wait()


def shards(current, owner, voxel, material, resist, green):
    values = [jnp.asarray(tables()[name]) for name in NAMES]
    vmem, smem, anywhere = (
        pl.BlockSpec(memory_space=space) for space in (pltpu.VMEM, pltpu.SMEM, pl.ANY)
    )
    dma = pltpu.SemaphoreType.DMA
    shapes = [
        ((3, 2, 32, 4096), F32),
        ((256, LANES), F32),
        ((256, LANES), F32),
        ((2048, LANES), F32),
        ((2048, LANES), F32),
        ((2048, LANES), F32),
        ((2048, LANES), F32),
        ((128, LANES), F32),
        ((128, LANES), F32),
        ((512, 256), F32),
        ((ROWS, 256, 2048), BF16),
        ((1024, 768), BF16),
        ((4096, LANES), F32),
        ((4096, LANES), F32),
        ((4, 4096, LANES), F32),
    ] + [(value.shape, value.dtype) for value in values]
    return pl.pallas_call(
        kernel,
        out_shape=jax.ShapeDtypeStruct(current.shape, F32),
        in_specs=[smem, smem, vmem, vmem, vmem, anywhere] + [anywhere] * len(values),
        out_specs=vmem,
        scratch_shapes=[pltpu.VMEM(*shape) for shape in shapes]
        + [
            dma((len(values) + 1,)),
            dma((4,)),
            dma((ROWS,)),
            dma((EDGE,)),
            dma,
            dma,
            pltpu.SemaphoreType.REGULAR,
        ],
        compiler_params=pltpu.CompilerParams(
            collective_id=0, has_side_effects=True, vmem_limit_bytes=58 * 1024 * 1024
        ),
    )(owner, resist, current, voxel, material, green, *values)


def solution(mesh):
    in_specs = (
        P(("row", "col"), None),
        P(("row", "col")),
        P(("row", "col"), None),
        P(("row", "col"), None),
        P(),
        P(None, None, ("row", "col"), None),
    )
    out_specs = P(("row", "col"), None)
    return jax.shard_map(shards, mesh=mesh, in_specs=in_specs, out_specs=out_specs, check_vma=False)
```

time: 164 us -> 83.6 us (0.51)
  blocking collectives: 101 us -> 0 us
  Pallas kernels: 62.4 us -> 81.8 us
    all_to_all x5 -> x0, blocking collectives: 101 us -> none  [the longest x2 36.8 us: shards(): values, places = (swap(values), swap(places))]
    pallas_call x5 -> x1, Pallas kernels: 62.4 us -> 81.8 us  [shards(): pl.pallas_call(kernel, out_shape=jax.ShapeDtypeStruct(current.shape, F32)...]
where the time goes in v2:
time: 83.6 us; the launch traced here: 83.1 us
  Pallas kernels  81.8 us (98%)
  local copies, waits for them, and re-layouts  1.32 us (2%)
    pallas_call x1, Pallas kernels, shards(): pl.pallas_call(kernel, out_shape=jax.ShapeDtypeStruct(current.shape, F32)...  81.8 us

profile of v2, /device:TPU:1, one launch (start us, length us, event | category | flops | bytes accessed | tf_op | source)
XLA Modules:
  0.0 83.1 jit_solution(18237495073111909867)
XLA Ops:
  0.0 81.8 %shard_map.145 = f32[32,128]{1,0:T(8,128)} custom-call(s32[32]{0:T(128)} %owner_ref.1, f32[8]{0:T(128)} %resist_ref.1, f32[32,128]{1,0:T(8,128)} %current_ref.1, s32[32,128]{1,0:T(8,128)} %voxel_ref.1, s32[32,128]{1,0:T(8,128)} %material_ref.1, f32[3,2,32,4096]{3,2,1,0:T(8,128)} %green_hbm.1, bf16[64,48]{1,0:T(8,128)(2,1)} %constant.18.clone.rest_0_, ...), custom_call_target="tpu_custom_call" | custom-call | tf_op jit(solution)/shard_map/pallas_call | solution.py:389
  81.8 1.3 %copy.17 = f32[32,128]{1,0:T(8,128)} copy(f32[32,128]{1,0:T(8,128)} %shard_map.145) | data formatting | bytes 32768

commit v3 on v2

v3 whole, which is shorter than its diff:
```python
import functools
import math

import jax
import jax.numpy as jnp
import ml_dtypes
import numpy as np
from jax import lax
from jax.experimental import pallas as pl
from jax.experimental.pallas import tpu as pltpu
from jax.sharding import PartitionSpec as P

F32 = jnp.float32
BF16 = jnp.bfloat16
LANES = 128


def halves(table):
    high = table.astype(ml_dtypes.bfloat16)
    low = (table - high.astype(np.float64)).astype(ml_dtypes.bfloat16)
    return high, low


def stacked(table, axis):
    high, low = halves(table)
    return np.concatenate([high, high, low], axis=axis)


def angles(left, right, length):
    return 2.0 * math.pi * (np.outer(left, right) % length) / length


@functools.lru_cache(maxsize=None)
def tables():
    out = {}
    j32, a16, n128, n64, a32 = (np.arange(n) for n in (32, 16, 128, 64, 32))
    theta = angles(j32, a16, 32)
    out["y_first"] = stacked(np.concatenate([np.cos(theta), -np.sin(theta)], axis=0), 1)
    theta = angles(j32, n128, 4096)
    out["y_turn"] = np.stack([np.cos(theta), -np.sin(theta)]).astype(np.float32)
    theta = angles(n128, n128, 128)
    cosine, sine = np.cos(theta), np.sin(theta)
    out["y_second"] = stacked(np.block([[cosine, -sine], [sine, cosine]]), 0)
    out["y_back"] = stacked(np.concatenate([cosine, sine], axis=0), 1)
    theta = np.tile(angles(n128, j32, 4096), (1, 4))
    sign = np.where(np.arange(128) < 64, -1.0, 1.0)
    out["y_unturn"] = np.stack([np.cos(theta), np.sin(theta) * sign]).astype(np.float32)
    theta = angles(j32, a16, 32)
    last = np.zeros((4, 2, 2, 32, 4, 2, 16))
    for x in range(4):
        for z in range(2):
            last[x, 0, z, :, x, z, :] = np.cos(theta)
            last[x, 1, z, :, x, z, :] = -np.sin(theta)
    out["y_last"] = stacked(last.reshape(512, 128), 0)
    first = []
    final = []
    for b in range(64):
        theta = angles(n64, 64 * a32 + b, 4096)
        first.append(stacked(np.concatenate([np.cos(theta), np.sin(theta)], axis=0), 1))
        final.append(stacked(np.concatenate([np.cos(theta.T), np.sin(theta.T)], axis=0), 1))
    out["x_first"] = np.concatenate(first, axis=0)
    out["x_final"] = np.concatenate(final, axis=0)
    theta = angles(n64, n64, 64)
    out["x_mid"] = stacked(np.concatenate([np.cos(theta), np.sin(theta)], axis=0), 1)
    return out


def split(value):
    high = value.astype(BF16)
    return high, (value - high.astype(F32)).astype(BF16)


MESH = pl.DeviceIdType.MESH
ROWS, COLS, EDGE = 8, 16, 4
NAMES = (
    "y_first", "y_turn", "y_second", "x_first", "x_mid", "x_final", "y_back", "y_unturn", "y_last",
)


def dot(left, right, dims=(((1,), (0,)), ((), ()))):
    return lax.dot_general(left, right, dims, preferred_element_type=F32)


def triple(value):
    high, low = split(value)
    return jnp.concatenate([high, low, high], axis=0)


def combine(product, place, low):
    count = product.shape[0] // 2
    cosine = product[:count, LANES * place : LANES * place + LANES]
    sine = product[count:, LANES * place : LANES * place + LANES]
    lane = lax.broadcasted_iota(jnp.int32, (count, LANES), 1)
    sign = jnp.where(lane < LANES // 2, low, -low).astype(F32)
    return cosine + pltpu.roll(sine, LANES // 2, 1) * sign


def aligned(value, step):
    return pl.multiple_of(value * step, step)


def kernel(
    owner_ref, resist_ref, current_ref, voxel_ref, material_ref, green_hbm, *rest
):
    count = len(NAMES)
    tables_hbm, out_ref = rest[:count], rest[count]
    (
        green_ref, route_out, route_in, spread_ref, pencil_ref, field_out, field_in, picked_ref, returned_ref,
        slab_ref, top_ref, left_ref, half_ref, back_ref, coef_ref, volume_ref,
    ) = rest[count + 1 : count + 17]
    held = rest[count + 17 : 2 * count + 17]
    load_sems, send_sems, route_sems, pencil_sems, field_sems, return_sem, spread_gate = rest[2 * count + 17 :]
    first_y, turn_ref, second_y, first_x, mid_x, final_x, back_y, unturn_ref, last_y = held

    row, col = lax.axis_index("row"), lax.axis_index("col")
    me = row * COLS + col
    high_col, low_col = lax.div(col, EDGE), lax.rem(col, EDGE)

    barrier = pltpu.get_barrier_semaphore()
    for k in range(1, ROWS):
        pl.semaphore_signal(barrier, inc=1, device_id=(lax.rem(row + k, ROWS), col), device_id_type=MESH)
    for k in range(1, COLS):
        pl.semaphore_signal(barrier, inc=1, device_id=(row, lax.rem(col + k, COLS)), device_id_type=MESH)

    loads = [pltpu.make_async_copy(green_hbm, green_ref, load_sems.at[count])]
    loads += [pltpu.make_async_copy(tables_hbm[i], held[i], load_sems.at[i]) for i in range(count)]
    for load in loads:
        load.start()

    voxel = voxel_ref[...]
    live = voxel >= 0
    loaded = jnp.where(live, current_ref[...], 0.0)
    cells = voxel.astype(F32)
    values = jnp.zeros((ROWS * COLS, LANES), F32)
    places = jnp.full((ROWS * COLS, LANES), -1.0, F32)
    ids = lax.broadcasted_iota(jnp.int32, values.shape, 0)
    for block in range(current_ref.shape[0]):
        mine = ids == owner_ref[block]
        values = jnp.where(mine, loaded[block : block + 1], values)
        places = jnp.where(mine, cells[block : block + 1], places)
    route_out[pl.ds(0, ROWS * COLS, stride=2), :] = values
    route_out[pl.ds(1, ROWS * COLS, stride=2), :] = places
    pl.semaphore_wait(barrier, ROWS + COLS - 2)
    for k in range(1, COLS):
        pl.semaphore_signal(spread_gate, inc=1, device_id=(row, lax.rem(col + k, COLS)), device_id_type=MESH)
    def remote(source, target, size, device, send_sem, recv_sem, start=0, pitch=None):
        pitch = pitch or size
        index = device[0] * COLS + device[1]
        return pltpu.make_async_remote_copy(
            source.at[pl.ds(index * pitch + start, size)],
            target.at[pl.ds(me * pitch + start, size)],
            send_sem,
            recv_sem,
            device_id=device,
            device_id_type=MESH,
        )

    def local(source, target, size, recv_sem, start=0, pitch=None):
        mine = pl.ds(me * (pitch or size) + start, size)
        return pltpu.make_async_copy(source.at[mine], target.at[mine], recv_sem)

    def arrival(ref, rows, sem):
        part = ref.at[pl.ds(0, rows)]
        pltpu.make_async_copy(part, part, sem).wait()

    far = (2, 1, 3, 0)
    far_cols = [
        lax.rem(high_col + y, EDGE) * EDGE + lax.rem(low_col + x, EDGE) for y in far for x in far if (y, x) != (0, 0)
    ]
    next_cols = [lax.rem(col + k, COLS) for k in range(1, COLS)]

    def route(to_row, to_col, r):
        remote(route_out, route_in, 2, (to_row, to_col), send_sems.at[0], route_sems.at[r]).start()

    for to_col in next_cols:
        route(row, to_col, 0)
    local(route_out, route_in, 2, route_sems.at[0]).start()
    for r in range(1, ROWS):
        route(lax.rem(row + r, ROWS), col, r)
    pl.semaphore_wait(spread_gate, COLS - 1)

    @pl.loop(1, ROWS)
    def _(r):
        to_row = lax.rem(row + r, ROWS)
        for to_col in next_cols:
            route(to_row, to_col, r)

    def to_all(send):
        @pl.loop(0, ROWS)
        def _(k):
            core = lax.rem(row + 1 + lax.div(k, 4), 2)
            to_row = 2 * lax.rem(lax.div(row, 2) + 2 + 3 * lax.rem(k, 4), 4) + core
            for to_col in far_cols:
                send((to_row, to_col))

            @pl.when(to_row != row)
            def _():
                send((to_row, col))

    side = lax.broadcasted_iota(jnp.int32, (256, LANES), 0).astype(F32).astype(BF16)
    one, zero = jnp.ones((256, LANES), BF16), jnp.zeros((256, LANES), BF16)

    def asked(step):
        block = route_in[pl.ds(aligned(lax.rem(row - step + ROWS, ROWS), 2 * COLS), 2 * COLS), :]
        return block, block.astype(jnp.int32)

    for half in range(2):
        slab_ref[...] = jnp.zeros_like(slab_ref)

        @pl.loop(0, ROWS)
        def _(step):
            if half == 0:
                arrival(route_in, 2 * COLS, route_sems.at[step])
            block, place = asked(step)
            top = jnp.where(place < 0, -1, (place >> 7) & 255).astype(F32).astype(BF16)
            spot = jnp.where((place >> 15) == half, place & 127, -1).astype(F32).astype(BF16)
            high, low = split(block)
            spots = []
            for s in range(COLS):
                if half == 0:
                    top_ref[step, :, LANES * s : LANES * s + LANES] = jnp.where(
                        side == top[2 * s + 1 : 2 * s + 2], one, zero
                    )
                hit = side[:LANES] == spot[2 * s + 1 : 2 * s + 2]
                spots.append(
                    jnp.concatenate(
                        [
                            jnp.where(hit, high[2 * s : 2 * s + 1], zero[:LANES]),
                            jnp.where(hit, low[2 * s : 2 * s + 1], zero[:LANES]),
                        ],
                        axis=0,
                    )
                )
            slab_ref[...] += dot(jnp.concatenate(spots, axis=1), top_ref[step], (((1,), (1,)), ((), ())))

        if half == 0:
            for load in loads[1:]:
                load.wait()
        slab = (slab_ref[:LANES, :] + slab_ref[LANES:, :]).T
        wide = jnp.concatenate([slab[16 * i : 16 * i + 16] for i in range(16)], axis=1)
        begun = dot(first_y[...], triple(wide))
        turn_re, turn_im = turn_ref[0], turn_ref[1]
        for i in range(16):
            re = begun[:32, LANES * i : LANES * i + LANES]
            im = begun[32:, LANES * i : LANES * i + LANES]
            both = jnp.concatenate([re * turn_re - im * turn_im, re * turn_im + im * turn_re], axis=1)
            high, low = split(both)
            left_ref[32 * i : 32 * i + 32, :] = jnp.concatenate([high, low, high], axis=1)
        spectra = dot(left_ref[...], second_y[...])
        for x in range(8):
            part = spectra[64 * x : 64 * x + 64]
            part = jnp.concatenate([part[:, :LANES], part[:, LANES:]], axis=0)
            spread_ref[pl.ds(8 * half + x, LANES, stride=16), :] = part.T

        def send(device):
            remote(
                spread_ref, pencil_ref, 8, device, send_sems.at[1 + half], pencil_sems.at[half], 8 * half, 16
            ).start()

        to_all(send)
        local(spread_ref, pencil_ref, 8, pencil_sems.at[half], 8 * half, 16).start()

    loads[0].wait()

    @pl.loop(0, 32)
    def _(tile):
        cols = pl.ds(aligned(tile, LANES), LANES)
        re = [green_ref[o, 0, :, cols] for o in range(3)]
        im = [green_ref[o, 1, :, cols] for o in range(3)]
        arranged = [
            [re[1], re[1], re[1], re[1]],
            [re[0], -im[2], re[0], im[2]],
            [-im[1], -im[1], im[1], im[1]],
            [-im[0], re[2], im[0], re[2]],
        ]
        for g in range(4):
            turned = jnp.concatenate(arranged[g], axis=0).T
            coef_ref[g, pl.ds(2 * tile, 64, stride=64), :] = turned[:64]
            coef_ref[g, pl.ds(2 * tile + 1, 64, stride=64), :] = turned[64:]

    for half in range(2):
        arrival(pencil_ref, 1024, pencil_sems.at[half])
        for b in range(64):
            if (b % 16) // 8 == half:
                rows = pencil_ref[pl.ds(b, 32, stride=64), :]
                product = dot(first_x[128 * b : 128 * b + 128, :], triple(rows))
                half_ref[pl.ds(b, 64, stride=64), :] = combine(product, 0, 1.0)

    mid = mid_x[...]
    for start in range(0, 64, 8):
        ks = range(start, start + 8)
        product = dot(
            mid, jnp.concatenate([triple(half_ref[64 * k : 64 * k + 64, :]) for k in ks], axis=1)
        )
        mixed = []
        for i, k in enumerate(ks):
            spectrum = combine(product, i, 1.0)
            total = coef_ref[0, 64 * k : 64 * k + 64, :] * spectrum
            for g in range(1, 4):
                total = total + coef_ref[g, 64 * k : 64 * k + 64, :] * pltpu.roll(spectrum, LANES - 32 * g, 1)
            mixed.append(triple(total))
        product = dot(mid, jnp.concatenate(mixed, axis=1))
        for i, k in enumerate(ks):
            back_ref[pl.ds(k, 64, stride=64), :] = combine(product, i, -1.0)

    for half in range(2):
        for b in range(64):
            if (b % 16) // 8 == half:
                product = dot(final_x[64 * b : 64 * b + 64, :], triple(back_ref[64 * b : 64 * b + 64, :]))
                field_out[pl.ds(b, 32, stride=64), :] = combine(product, 0, -1.0)

        def send(device):
            remote(
                field_out, field_in, 8, device, send_sems.at[3 + half], field_sems.at[half], 8 * half, 16
            ).start()

        to_all(send)
        local(field_out, field_in, 8, field_sems.at[half], 8 * half, 16).start()

    cosine, sine = unturn_ref[0], unturn_ref[1]
    spots = lax.broadcasted_iota(jnp.int32, (LANES, LANES), 0)
    for half in range(2):
        arrival(field_in, 1024, field_sems.at[half])
        back = back_y[...]
        pieces = []
        for quad in range(2 * half, 2 * half + 2):
            product = dot(
                back,
                jnp.concatenate(
                    [triple(field_in[pl.ds(4 * quad + i, LANES, stride=16), :]) for i in range(4)], axis=1
                ),
            )
            turned = []
            for i in range(4):
                piece = combine(product, i, -1.0)
                turned.append(piece * cosine + pltpu.roll(piece, LANES // 2, 1) * sine)
            high, low = split(jnp.concatenate(turned, axis=1))
            pieces.append(dot(jnp.concatenate([high, low, high], axis=1), last_y[...]))
        volume_ref[...] = jnp.concatenate(split(jnp.concatenate(pieces, axis=1) * (1.0 / 16777216.0)), axis=0)

        @pl.loop(0, ROWS)
        def _(step):
            base = lax.rem(row - step + ROWS, ROWS)
            block, place = asked(step)
            spot = jnp.where((place >> 15) == half, place & 127, -1)
            found = dot(volume_ref[...], top_ref[step])
            lines = []
            for s in range(COLS):
                line = found[:LANES, LANES * s : LANES * s + LANES] + found[LANES:, LANES * s : LANES * s + LANES]
                line = jnp.where(spots == spot[2 * s + 1 : 2 * s + 2], line, 0.0)
                lines.append(jnp.sum(line, axis=0, keepdims=True))
            lines = jnp.concatenate(lines, axis=0)
            rows = pl.ds(aligned(base, COLS), COLS)
            if half == 0:
                picked_ref[rows, :] = lines
            else:
                picked_ref[rows, :] += lines

                @pl.when(step == 0)
                def _():
                    local(picked_ref, returned_ref, 1, return_sem).start()

                for to_col in next_cols:
                    remote(picked_ref, returned_ref, 1, (base, to_col), send_sems.at[5], return_sem).start()

                @pl.when(step > 0)
                def _():
                    remote(picked_ref, returned_ref, 1, (base, col), send_sems.at[5], return_sem).start()

    rates = jnp.zeros(current_ref.shape, F32)
    for kind in range(8):
        rates = jnp.where(material_ref[...] == kind, resist_ref[kind], rates)
    own = rates * current_ref[...]
    pltpu.make_async_copy(returned_ref, returned_ref, return_sem).wait()
    coupled = jnp.concatenate(
        [returned_ref[pl.ds(owner_ref[b], 1), :] for b in range(current_ref.shape[0])], axis=0
    )
    out_ref[...] = jnp.where(live, own + coupled, 0.0)
    for i, (ref, size) in enumerate(
        ((route_out, 2), (spread_ref, 8), (spread_ref, 8), (field_out, 8), (field_out, 8), (picked_ref, 1))
    ):
        arrival(ref, (ROWS * COLS - 1) * size, send_sems.at[i])


def shards(current, owner, voxel, material, resist, green):
    values = [jnp.asarray(tables()[name]) for name in NAMES]
    vmem, smem, anywhere = (
        pl.BlockSpec(memory_space=space) for space in (pltpu.VMEM, pltpu.SMEM, pl.ANY)
    )
    dma = pltpu.SemaphoreType.DMA
    shapes = [
        ((3, 2, 32, 4096), F32),
        ((256, LANES), F32),
        ((256, LANES), F32),
        ((2048, LANES), F32),
        ((2048, LANES), F32),
        ((2048, LANES), F32),
        ((2048, LANES), F32),
        ((128, LANES), F32),
        ((128, LANES), F32),
        ((256, 256), F32),
        ((ROWS, 256, 2048), BF16),
        ((512, 768), BF16),
        ((4096, LANES), F32),
        ((4096, LANES), F32),
        ((4, 4096, LANES), F32),
        ((256, 256), BF16),
    ] + [(value.shape, value.dtype) for value in values]
    return pl.pallas_call(
        kernel,
        out_shape=jax.ShapeDtypeStruct(current.shape, F32),
        in_specs=[smem, smem, vmem, vmem, vmem, anywhere] + [anywhere] * len(values),
        out_specs=vmem,
        scratch_shapes=[pltpu.VMEM(*shape) for shape in shapes]
        + [
            dma((len(values) + 1,)),
            dma((6,)),
            dma((ROWS,)),
            dma((2,)),
            dma((2,)),
            dma,
            pltpu.SemaphoreType.REGULAR,
        ],
        compiler_params=pltpu.CompilerParams(
            collective_id=0, has_side_effects=True, vmem_limit_bytes=58 * 1024 * 1024
        ),
    )(owner, resist, current, voxel, material, green, *values)


def solution(mesh):
    in_specs = (
        P(("row", "col"), None),
        P(("row", "col")),
        P(("row", "col"), None),
        P(("row", "col"), None),
        P(),
        P(None, None, ("row", "col"), None),
    )
    out_specs = P(("row", "col"), None)
    return jax.shard_map(shards, mesh=mesh, in_specs=in_specs, out_specs=out_specs, check_vma=False)
```

time: 83.6 us -> 77.3 us (0.925)
  Pallas kernels: 81.8 us -> 75.7 us
    pallas_call x1, Pallas kernels: 81.8 us -> 75.7 us  [shards(): pl.pallas_call(kernel, out_shape=jax.ShapeDtypeStruct(current.shape, F32)...]
where the time goes in v3:
time: 77.3 us; the launch traced here: 77.1 us
  Pallas kernels  75.7 us (98%)
  local copies, waits for them, and re-layouts  1.32 us (2%)
    pallas_call x1, Pallas kernels, shards(): pl.pallas_call(kernel, out_shape=jax.ShapeDtypeStruct(current.shape, F32)...  75.7 us

profile of v3, /device:TPU:1, one launch (start us, length us, event | category | flops | bytes accessed | tf_op | source)
XLA Modules:
  0.0 77.1 jit_solution(15913017344947279563)
XLA Ops:
  0.0 75.7 %shard_map.145 = f32[32,128]{1,0:T(8,128)} custom-call(s32[32]{0:T(128)} %owner_ref.1, f32[8]{0:T(128)} %resist_ref.1, f32[32,128]{1,0:T(8,128)} %current_ref.1, s32[32,128]{1,0:T(8,128)} %voxel_ref.1, s32[32,128]{1,0:T(8,128)} %material_ref.1, f32[3,2,32,4096]{3,2,1,0:T(8,128)} %green_hbm.1, bf16[64,48]{1,0:T(8,128)(2,1)} %constant.18.clone.rest_0_, ...), custom_call_target="tpu_custom_call" | custom-call | tf_op jit(solution)/shard_map/pallas_call | solution.py:409
  75.8 1.3 %copy.17 = f32[32,128]{1,0:T(8,128)} copy(f32[32,128]{1,0:T(8,128)} %shard_map.145) | data formatting | bytes 32768

commit v4 on v3

--- a/solution.py
+++ b/solution.py
@@ -72,6 +72,7 @@
 
 MESH = pl.DeviceIdType.MESH
 ROWS, COLS, EDGE = 8, 16, 4
+PITCH, BLOCK = 72, 24
 NAMES = (
     "y_first", "y_turn", "y_second", "x_first", "x_mid", "x_final", "y_back", "y_unturn", "y_last",
 )
@@ -143,21 +144,27 @@
     pl.semaphore_wait(barrier, ROWS + COLS - 2)
     for k in range(1, COLS):
         pl.semaphore_signal(spread_gate, inc=1, device_id=(row, lax.rem(col + k, COLS)), device_id_type=MESH)
-    def remote(source, target, size, device, send_sem, recv_sem, start=0, pitch=None):
-        pitch = pitch or size
-        index = device[0] * COLS + device[1]
+    def remote(source, start, target, place, size, device, send_sem, recv_sem):
         return pltpu.make_async_remote_copy(
-            source.at[pl.ds(index * pitch + start, size)],
-            target.at[pl.ds(me * pitch + start, size)],
+            source.at[pl.ds(start, size)],
+            target.at[pl.ds(place, size)],
             send_sem,
             recv_sem,
             device_id=device,
             device_id_type=MESH,
         )
 
-    def local(source, target, size, recv_sem, start=0, pitch=None):
-        mine = pl.ds(me * (pitch or size) + start, size)
-        return pltpu.make_async_copy(source.at[mine], target.at[mine], recv_sem)
+    def local(source, start, target, place, size, recv_sem):
+        return pltpu.make_async_copy(source.at[pl.ds(start, size)], target.at[pl.ds(place, size)], recv_sem)
+
+    def outward(k, middle):
+        return middle + (1 - 2 * lax.rem(k, 2)) * lax.div(k + 1, 2)
+
+    def in_row(to_col):
+        return lax.div(to_col, EDGE) * PITCH + lax.rem(to_col, EDGE) * 16
+
+    own_x = row * (EDGE * PITCH) + in_row(col)
+    own_block = me * BLOCK
 
     def arrival(ref, rows, sem):
         part = ref.at[pl.ds(0, rows)]
@@ -167,35 +174,39 @@
     far_cols = [
         lax.rem(high_col + y, EDGE) * EDGE + lax.rem(low_col + x, EDGE) for y in far for x in far if (y, x) != (0, 0)
     ]
+    far_places = [in_row(to_col) for to_col in far_cols]
+    own_place = in_row(col)
     next_cols = [lax.rem(col + k, COLS) for k in range(1, COLS)]
 
     def route(to_row, to_col, r):
-        remote(route_out, route_in, 2, (to_row, to_col), send_sems.at[0], route_sems.at[r]).start()
+        start = 2 * (to_row * COLS + to_col)
+        remote(route_out, start, route_in, 2 * me, 2, (to_row, to_col), send_sems.at[0], route_sems.at[r]).start()
 
     for to_col in next_cols:
         route(row, to_col, 0)
-    local(route_out, route_in, 2, route_sems.at[0]).start()
+    local(route_out, 2 * me, route_in, 2 * me, 2, route_sems.at[0]).start()
     for r in range(1, ROWS):
         route(lax.rem(row + r, ROWS), col, r)
     pl.semaphore_wait(spread_gate, COLS - 1)
 
-    @pl.loop(1, ROWS)
-    def _(r):
+    @pl.loop(0, ROWS - 1)
+    def _(k):
+        r = outward(k, ROWS // 2)
         to_row = lax.rem(row + r, ROWS)
-        for to_col in next_cols:
+        for to_col in far_cols:
             route(to_row, to_col, r)
 
     def to_all(send):
         @pl.loop(0, ROWS)
         def _(k):
             core = lax.rem(row + 1 + lax.div(k, 4), 2)
-            to_row = 2 * lax.rem(lax.div(row, 2) + 2 + 3 * lax.rem(k, 4), 4) + core
-            for to_col in far_cols:
-                send((to_row, to_col))
+            to_row = 2 * lax.rem(lax.div(row, 2) + outward(lax.rem(k, 4), 2), 4) + core
+            for to_col, place in zip(far_cols, far_places):
+                send(to_row, to_col, place)
 
             @pl.when(to_row != row)
             def _():
-                send((to_row, col))
+                send(to_row, col, own_place)
 
     side = lax.broadcasted_iota(jnp.int32, (256, LANES), 0).astype(F32).astype(BF16)
     one, zero = jnp.ones((256, LANES), BF16), jnp.zeros((256, LANES), BF16)
@@ -208,7 +219,8 @@
         slab_ref[...] = jnp.zeros_like(slab_ref)
 
         @pl.loop(0, ROWS)
-        def _(step):
+        def _(k):
+            step = lax.rem(outward(lax.rem(k + ROWS - 1, ROWS), ROWS // 2), ROWS)
             if half == 0:
                 arrival(route_in, 2 * COLS, route_sems.at[step])
             block, place = asked(step)
@@ -250,15 +262,20 @@
         for x in range(8):
             part = spectra[64 * x : 64 * x + 64]
             part = jnp.concatenate([part[:, :LANES], part[:, LANES:]], axis=0)
-            spread_ref[pl.ds(8 * half + x, LANES, stride=16), :] = part.T
-
-        def send(device):
+            spread_ref[pl.ds(8 * half + x, LANES, stride=BLOCK), :] = part.T
+
+        def send(to_row, to_col, place):
+            start = pl.multiple_of((to_row * COLS + to_col) * BLOCK + 8 * half, 8)
             remote(
-                spread_ref, pencil_ref, 8, device, send_sems.at[1 + half], pencil_sems.at[half], 8 * half, 16
+                spread_ref, start, pencil_ref, pl.multiple_of(own_x + 8 * half, 8), 8, (to_row, to_col),
+                send_sems.at[1 + half], pencil_sems.at[half],
             ).start()
 
         to_all(send)
-        local(spread_ref, pencil_ref, 8, pencil_sems.at[half], 8 * half, 16).start()
+        local(
+            spread_ref, pl.multiple_of(own_block + 8 * half, 8), pencil_ref, pl.multiple_of(own_x + 8 * half, 8), 8,
+            pencil_sems.at[half],
+        ).start()
 
     loads[0].wait()
 
@@ -275,47 +292,52 @@
         ]
         for g in range(4):
             turned = jnp.concatenate(arranged[g], axis=0).T
-            coef_ref[g, pl.ds(2 * tile, 64, stride=64), :] = turned[:64]
-            coef_ref[g, pl.ds(2 * tile + 1, 64, stride=64), :] = turned[64:]
+            coef_ref[g, pl.ds(2 * tile, 64, stride=PITCH), :] = turned[:64]
+            coef_ref[g, pl.ds(2 * tile + 1, 64, stride=PITCH), :] = turned[64:]
 
     for half in range(2):
         arrival(pencil_ref, 1024, pencil_sems.at[half])
         for b in range(64):
             if (b % 16) // 8 == half:
-                rows = pencil_ref[pl.ds(b, 32, stride=64), :]
+                rows = pencil_ref[pl.ds(b, 32, stride=PITCH), :]
                 product = dot(first_x[128 * b : 128 * b + 128, :], triple(rows))
-                half_ref[pl.ds(b, 64, stride=64), :] = combine(product, 0, 1.0)
+                half_ref[pl.ds(b, 64, stride=PITCH), :] = combine(product, 0, 1.0)
 
     mid = mid_x[...]
     for start in range(0, 64, 8):
         ks = range(start, start + 8)
         product = dot(
-            mid, jnp.concatenate([triple(half_ref[64 * k : 64 * k + 64, :]) for k in ks], axis=1)
+            mid, jnp.concatenate([triple(half_ref[PITCH * k : PITCH * k + 64, :]) for k in ks], axis=1)
         )
         mixed = []
         for i, k in enumerate(ks):
             spectrum = combine(product, i, 1.0)
-            total = coef_ref[0, 64 * k : 64 * k + 64, :] * spectrum
+            total = coef_ref[0, PITCH * k : PITCH * k + 64, :] * spectrum
             for g in range(1, 4):
-                total = total + coef_ref[g, 64 * k : 64 * k + 64, :] * pltpu.roll(spectrum, LANES - 32 * g, 1)
+                total = total + coef_ref[g, PITCH * k : PITCH * k + 64, :] * pltpu.roll(spectrum, LANES - 32 * g, 1)
             mixed.append(triple(total))
         product = dot(mid, jnp.concatenate(mixed, axis=1))
         for i, k in enumerate(ks):
-            back_ref[pl.ds(k, 64, stride=64), :] = combine(product, i, -1.0)
+            back_ref[pl.ds(k, 64, stride=PITCH), :] = combine(product, i, -1.0)
 
     for half in range(2):
         for b in range(64):
             if (b % 16) // 8 == half:
-                product = dot(final_x[64 * b : 64 * b + 64, :], triple(back_ref[64 * b : 64 * b + 64, :]))
-                field_out[pl.ds(b, 32, stride=64), :] = combine(product, 0, -1.0)
-
-        def send(device):
+                product = dot(final_x[64 * b : 64 * b + 64, :], triple(back_ref[PITCH * b : PITCH * b + 64, :]))
+                field_out[pl.ds(b, 32, stride=PITCH), :] = combine(product, 0, -1.0)
+
+        def send(to_row, to_col, place):
+            start = pl.multiple_of(to_row * (EDGE * PITCH) + place + 8 * half, 8)
             remote(
-                field_out, field_in, 8, device, send_sems.at[3 + half], field_sems.at[half], 8 * half, 16
+                field_out, start, field_in, pl.multiple_of(own_block + 8 * half, 8), 8, (to_row, to_col),
+                send_sems.at[3 + half], field_sems.at[half],
             ).start()
 
         to_all(send)
-        local(field_out, field_in, 8, field_sems.at[half], 8 * half, 16).start()
+        local(
+            field_out, pl.multiple_of(own_x + 8 * half, 8), field_in, pl.multiple_of(own_block + 8 * half, 8), 8,
+            field_sems.at[half],
+        ).start()
 
     cosine, sine = unturn_ref[0], unturn_ref[1]
     spots = lax.broadcasted_iota(jnp.int32, (LANES, LANES), 0)
@@ -327,7 +349,7 @@
             product = dot(
                 back,
                 jnp.concatenate(
-                    [triple(field_in[pl.ds(4 * quad + i, LANES, stride=16), :]) for i in range(4)], axis=1
+                    [triple(field_in[pl.ds(4 * quad + i, LANES, stride=BLOCK), :]) for i in range(4)], axis=1
                 ),
             )
             turned = []
@@ -339,7 +361,8 @@
         volume_ref[...] = jnp.concatenate(split(jnp.concatenate(pieces, axis=1) * (1.0 / 16777216.0)), axis=0)
 
         @pl.loop(0, ROWS)
-        def _(step):
+        def _(k):
+            step = outward(k, ROWS // 2)
             base = lax.rem(row - step + ROWS, ROWS)
             block, place = asked(step)
             spot = jnp.where((place >> 15) == half, place & 127, -1)
@@ -356,16 +379,20 @@
             else:
                 picked_ref[rows, :] += lines
 
-                @pl.when(step == 0)
+                @pl.when(k == ROWS - 1)
                 def _():
-                    local(picked_ref, returned_ref, 1, return_sem).start()
-
-                for to_col in next_cols:
-                    remote(picked_ref, returned_ref, 1, (base, to_col), send_sems.at[5], return_sem).start()
-
-                @pl.when(step > 0)
+                    local(picked_ref, me, returned_ref, me, 1, return_sem).start()
+
+                for to_col in far_cols:
+                    remote(
+                        picked_ref, base * COLS + to_col, returned_ref, me, 1, (base, to_col), send_sems.at[5], return_sem
+                    ).start()
+
+                @pl.when(k < ROWS - 1)
                 def _():
-                    remote(picked_ref, returned_ref, 1, (base, col), send_sems.at[5], return_sem).start()
+                    remote(
+                        picked_ref, base * COLS + col, returned_ref, me, 1, (base, col), send_sems.at[5], return_sem
+                    ).start()
 
     rates = jnp.zeros(current_ref.shape, F32)
     for kind in range(8):
@@ -392,18 +419,18 @@
         ((3, 2, 32, 4096), F32),
         ((256, LANES), F32),
         ((256, LANES), F32),
-        ((2048, LANES), F32),
-        ((2048, LANES), F32),
-        ((2048, LANES), F32),
-        ((2048, LANES), F32),
+        ((128 * BLOCK, LANES), F32),
+        ((32 * PITCH, LANES), F32),
+        ((32 * PITCH, LANES), F32),
+        ((128 * BLOCK, LANES), F32),
         ((128, LANES), F32),
         ((128, LANES), F32),
         ((256, 256), F32),
         ((ROWS, 256, 2048), BF16),
         ((512, 768), BF16),
-        ((4096, LANES), F32),
-        ((4096, LANES), F32),
-        ((4, 4096, LANES), F32),
+        ((64 * PITCH, LANES), F32),
+        ((64 * PITCH, LANES), F32),
+        ((4, 64 * PITCH, LANES), F32),
         ((256, 256), BF16),
     ] + [(value.shape, value.dtype) for value in values]
     return pl.pallas_call(

time: 77.3 us -> 71.5 us (0.925)
  Pallas kernels: 75.7 us -> 69.9 us
    pallas_call x1, Pallas kernels: 75.7 us -> 69.9 us  [shards(): pl.pallas_call(kernel, out_shape=jax.ShapeDtypeStruct(current.shape, F32)...]
where the time goes in v4:
time: 71.5 us; the launch traced here: 71.3 us
  Pallas kernels  69.9 us (98%)
  local copies, waits for them, and re-layouts  1.32 us (2%)
    pallas_call x1, Pallas kernels, shards(): pl.pallas_call(kernel, out_shape=jax.ShapeDtypeStruct(current.shape, F32)...  69.9 us

profile of v4, /device:TPU:1, one launch (start us, length us, event | category | flops | bytes accessed | tf_op | source)
XLA Modules:
  0.0 71.3 jit_solution(13386987721313293875)
XLA Ops:
  0.0 69.9 %shard_map.145 = f32[32,128]{1,0:T(8,128)} custom-call(s32[32]{0:T(128)} %owner_ref.1, f32[8]{0:T(128)} %resist_ref.1, f32[32,128]{1,0:T(8,128)} %current_ref.1, s32[32,128]{1,0:T(8,128)} %voxel_ref.1, s32[32,128]{1,0:T(8,128)} %material_ref.1, f32[3,2,32,4096]{3,2,1,0:T(8,128)} %green_hbm.1, bf16[64,48]{1,0:T(8,128)(2,1)} %constant.18.clone.rest_0_, ...), custom_call_target="tpu_custom_call" | custom-call | tf_op jit(solution)/shard_map/pallas_call | solution.py:436
  69.9 1.3 %copy.17 = f32[32,128]{1,0:T(8,128)} copy(f32[32,128]{1,0:T(8,128)} %shard_map.145) | data formatting | bytes 32768

commit v5 on v4

--- a/solution.py
+++ b/solution.py
@@ -110,7 +110,7 @@
         slab_ref, top_ref, left_ref, half_ref, back_ref, coef_ref, volume_ref,
     ) = rest[count + 1 : count + 17]
     held = rest[count + 17 : 2 * count + 17]
-    load_sems, send_sems, route_sems, pencil_sems, field_sems, return_sem, spread_gate = rest[2 * count + 17 :]
+    load_sems, send_sems, route_sems, pencil_sems, field_sems, return_sem = rest[2 * count + 17 :]
     first_y, turn_ref, second_y, first_x, mid_x, final_x, back_y, unturn_ref, last_y = held
 
     row, col = lax.axis_index("row"), lax.axis_index("col")
@@ -118,10 +118,13 @@
     high_col, low_col = lax.div(col, EDGE), lax.rem(col, EDGE)
 
     barrier = pltpu.get_barrier_semaphore()
-    for k in range(1, ROWS):
-        pl.semaphore_signal(barrier, inc=1, device_id=(lax.rem(row + k, ROWS), col), device_id_type=MESH)
-    for k in range(1, COLS):
-        pl.semaphore_signal(barrier, inc=1, device_id=(row, lax.rem(col + k, COLS)), device_id_type=MESH)
+    far = (2, 1, 3, 0)
+    all_cols = [lax.rem(high_col + y, EDGE) * EDGE + lax.rem(low_col + x, EDGE) for y in far for x in far]
+    far_cols = all_cols[:-1]
+    for r in (4, 3, 5, 2, 6, 1, 7, 0):
+        to_row = lax.rem(row + r, ROWS)
+        for to_col in all_cols if r else far_cols:
+            pl.semaphore_signal(barrier, inc=1, device_id=(to_row, to_col), device_id_type=MESH)
 
     loads = [pltpu.make_async_copy(green_hbm, green_ref, load_sems.at[count])]
     loads += [pltpu.make_async_copy(tables_hbm[i], held[i], load_sems.at[i]) for i in range(count)]
@@ -141,9 +144,8 @@
         places = jnp.where(mine, cells[block : block + 1], places)
     route_out[pl.ds(0, ROWS * COLS, stride=2), :] = values
     route_out[pl.ds(1, ROWS * COLS, stride=2), :] = places
-    pl.semaphore_wait(barrier, ROWS + COLS - 2)
-    for k in range(1, COLS):
-        pl.semaphore_signal(spread_gate, inc=1, device_id=(row, lax.rem(col + k, COLS)), device_id_type=MESH)
+    pl.semaphore_wait(barrier, ROWS * COLS - 1)
+
     def remote(source, start, target, place, size, device, send_sem, recv_sem):
         return pltpu.make_async_remote_copy(
             source.at[pl.ds(start, size)],
@@ -170,10 +172,6 @@
         part = ref.at[pl.ds(0, rows)]
         pltpu.make_async_copy(part, part, sem).wait()
 
-    far = (2, 1, 3, 0)
-    far_cols = [
-        lax.rem(high_col + y, EDGE) * EDGE + lax.rem(low_col + x, EDGE) for y in far for x in far if (y, x) != (0, 0)
-    ]
     far_places = [in_row(to_col) for to_col in far_cols]
     own_place = in_row(col)
     next_cols = [lax.rem(col + k, COLS) for k in range(1, COLS)]
@@ -187,7 +185,6 @@
     local(route_out, 2 * me, route_in, 2 * me, 2, route_sems.at[0]).start()
     for r in range(1, ROWS):
         route(lax.rem(row + r, ROWS), col, r)
-    pl.semaphore_wait(spread_gate, COLS - 1)
 
     @pl.loop(0, ROWS - 1)
     def _(k):
@@ -287,8 +284,8 @@
         arranged = [
             [re[1], re[1], re[1], re[1]],
             [re[0], -im[2], re[0], im[2]],
-            [-im[1], -im[1], im[1], im[1]],
-            [-im[0], re[2], im[0], re[2]],
+            [im[1], im[1], -im[1], -im[1]],
+            [im[0], re[2], -im[0], re[2]],
         ]
         for g in range(4):
             turned = jnp.concatenate(arranged[g], axis=0).T
@@ -312,9 +309,13 @@
         mixed = []
         for i, k in enumerate(ks):
             spectrum = combine(product, i, 1.0)
-            total = coef_ref[0, PITCH * k : PITCH * k + 64, :] * spectrum
-            for g in range(1, 4):
-                total = total + coef_ref[g, PITCH * k : PITCH * k + 64, :] * pltpu.roll(spectrum, LANES - 32 * g, 1)
+            aside = pltpu.roll(spectrum, LANES - 32, 1)
+            near, far_part = [
+                coef_ref[g, PITCH * k : PITCH * k + 64, :] * spectrum
+                + coef_ref[g + 1, PITCH * k : PITCH * k + 64, :] * aside
+                for g in (0, 2)
+            ]
+            total = near + pltpu.roll(far_part, LANES // 2, 1)
             mixed.append(triple(total))
         product = dot(mid, jnp.concatenate(mixed, axis=1))
         for i, k in enumerate(ks):
@@ -446,7 +447,6 @@
             dma((2,)),
             dma((2,)),
             dma,
-            pltpu.SemaphoreType.REGULAR,
         ],
         compiler_params=pltpu.CompilerParams(
             collective_id=0, has_side_effects=True, vmem_limit_bytes=58 * 1024 * 1024

time: 71.5 us -> 69.2 us (0.968)
  Pallas kernels: 69.9 us -> 67.5 us
    pallas_call x1, Pallas kernels: 69.9 us -> 67.5 us  [shards(): pl.pallas_call(kernel, out_shape=jax.ShapeDtypeStruct(current.shape, F32)...]
where the time goes in v5:
time: 69.2 us; the launch traced here: 68.9 us
  Pallas kernels  67.5 us (98%)
  local copies, waits for them, and re-layouts  1.32 us (2%)
    pallas_call x1, Pallas kernels, shards(): pl.pallas_call(kernel, out_shape=jax.ShapeDtypeStruct(current.shape, F32)...  67.5 us

profile of v5, /device:TPU:1, one launch (start us, length us, event | category | flops | bytes accessed | tf_op | source)
XLA Modules:
  0.0 68.9 jit_solution(17672399651803213514)
XLA Ops:
  0.0 67.5 %shard_map.145 = f32[32,128]{1,0:T(8,128)} custom-call(s32[32]{0:T(128)} %owner_ref.1, f32[8]{0:T(128)} %resist_ref.1, f32[32,128]{1,0:T(8,128)} %current_ref.1, s32[32,128]{1,0:T(8,128)} %voxel_ref.1, s32[32,128]{1,0:T(8,128)} %material_ref.1, f32[3,2,32,4096]{3,2,1,0:T(8,128)} %green_hbm.1, bf16[64,48]{1,0:T(8,128)(2,1)} %constant.18.clone.rest_0_, ...), custom_call_target="tpu_custom_call" | custom-call | tf_op jit(solution)/shard_map/pallas_call | solution.py:437
  67.6 1.3 %copy.17 = f32[32,128]{1,0:T(8,128)} copy(f32[32,128]{1,0:T(8,128)} %shard_map.145) | data formatting | bytes 32768

commit v6 on v5

--- a/solution.py
+++ b/solution.py
@@ -431,7 +431,7 @@
         ((512, 768), BF16),
         ((64 * PITCH, LANES), F32),
         ((64 * PITCH, LANES), F32),
-        ((4, 64 * PITCH, LANES), F32),
+        ((4, 65 * PITCH, LANES), F32),
         ((256, 256), BF16),
     ] + [(value.shape, value.dtype) for value in values]
     return pl.pallas_call(

time: 69.2 us -> 69.1 us (level)
  no operation moved by 1% of the time
where the time goes in v6:
time: 69.1 us; the launch traced here: 68.9 us
  Pallas kernels  67.5 us (98%)
  local copies, waits for them, and re-layouts  1.32 us (2%)
    pallas_call x1, Pallas kernels, shards(): pl.pallas_call(kernel, out_shape=jax.ShapeDtypeStruct(current.shape, F32)...  67.5 us

profile of v6, /device:TPU:1, one launch (start us, length us, event | category | flops | bytes accessed | tf_op | source)
XLA Modules:
  0.0 68.9 jit_solution(10249277941825943981)
XLA Ops:
  0.0 67.5 %shard_map.145 = f32[32,128]{1,0:T(8,128)} custom-call(s32[32]{0:T(128)} %owner_ref.1, f32[8]{0:T(128)} %resist_ref.1, f32[32,128]{1,0:T(8,128)} %current_ref.1, s32[32,128]{1,0:T(8,128)} %voxel_ref.1, s32[32,128]{1,0:T(8,128)} %material_ref.1, f32[3,2,32,4096]{3,2,1,0:T(8,128)} %green_hbm.1, bf16[64,48]{1,0:T(8,128)(2,1)} %constant.18.clone.rest_0_, ...), custom_call_target="tpu_custom_call" | custom-call | tf_op jit(solution)/shard_map/pallas_call | solution.py:437
  67.5 1.3 %copy.17 = f32[32,128]{1,0:T(8,128)} copy(f32[32,128]{1,0:T(8,128)} %shard_map.145) | data formatting | bytes 32768
